TPU v7x, 32 devices: a whole 2x2x4 slice. The times are simulated.
32 devices in a mesh: tp: 4 (over y, x), ep: 8 (over z, core).
Axes of the slice: x: 2, y: 2, z: 4, core: 2. Of those that a mesh axis runs over, the one named last changes fastest.
Arguments:
- tokens: bfloat16 [24576, 512], P(('ep', 'tp')), may hold values from -6 to 6
- lengths: int32 [24, 16], P('ep'), may hold values from 1 to 256, 1024 in all within a row
- task_ids: int32 [24, 16], P('ep'), may hold values from 0 to 29
- routes: int32 [24576, 2], P(('ep', 'tp')), may hold values from 0 to 7, all different within a row; in each aligned block of 768 rows (0 to 767, 768 to 1535, ...) at most 384 rows name the same one
- norm_gain: float32 [2, 512], replicated, may hold values from 0.1 to 1.9
- norm_bias: float32 [2, 512], replicated, may hold values from -3 to 3
- w_qkv: bfloat16 [512, 3, 512], P('ep', None, 'tp'), may hold values from -0.25 to 0.25
- w_out: bfloat16 [512, 512], P('ep', 'tp'), may hold values from -1.5 to 1.5
- w_router: bfloat16 [512, 8], replicated, may hold values from -0.125 to 0.125
- task_table: float32 [30, 8], replicated, may hold values from -3 to 3
- w_in: bfloat16 [8, 2048, 512], P('ep', 'tp'), may hold values from -0.25 to 0.25
- w_down: bfloat16 [8, 2048, 512], P('ep', 'tp'), may hold values from -0.125 to 0.125
- grad_out: bfloat16 [24576, 512], P(('ep', 'tp')), may hold values from -6 to 6
Outputs:
- mixed_out: bfloat16 [24576, 512], P(('ep', 'tp'))
- grad_tokens: bfloat16 [24576, 512], P(('ep', 'tp'))
- grad_gain: float32 [2, 512], replicated
- grad_bias: float32 [2, 512], replicated
- grad_qkv: float32 [512, 3, 512], P('ep', None, 'tp')
- grad_proj: float32 [512, 512], P('ep', 'tp')
- grad_router: float32 [512, 8], replicated
- grad_table: float32 [30, 8], replicated
- grad_in: float32 [8, 2048, 512], P('ep', 'tp')
- grad_down: float32 [8, 2048, 512], P('ep', 'tp')
Inputs may be any that keep to these rules, and one draw needn't show every extreme that they name: Each pack's 16 lengths sum to 1024, and the longest is 256 in every pack. `routes`: each row names two different experts; within the 768 rows of one device no expert is named by more than 384 rows, and in some device's rows one expert is named by exactly 384.
All inputs are finite; a program needn't handle non-finite values.
Results may differ from a plain program's by a relative error of at most 0.018.
The roundings to bfloat16 on the way count: a program that leaves them out, or rounds other values in their place, can miss the bound.
Values may be sent and summed in bfloat16 or wider, within the bound.
A program may use at most 192 MiB of HBM per device.

v0:
```python
import jax
import jax.numpy as jnp
from jax import lax
from jax.sharding import PartitionSpec as P

HEAD_DIM = 64
PACK = 1024


EPSILON = 1e-05
NEG_FILL = -1e30


def layer_norm(inputs, gain_row, bias_row):
    row_mean = jnp.mean(inputs, -1, keepdims=True)
    centred = inputs - row_mean
    row_var = jnp.mean(centred * centred, -1, keepdims=True)
    return centred * lax.rsqrt(row_var + EPSILON) * gain_row + bias_row


def pack_segments(lengths):
    sentence_ends = jnp.cumsum(lengths, axis=-1)
    places = jnp.arange(PACK, dtype=jnp.int32)
    return jnp.sum((places[None, :, None] >= sentence_ends[:, None, :]).astype(jnp.int32), -1)


def masked_scores(queries, key_part, segment):
    scores = jnp.einsum("ihd,jhd->hij", queries, key_part, preferred_element_type=jnp.float32)
    same_doc = segment[:, None] == segment[None, :]
    return jnp.where(same_doc[None], scores, NEG_FILL)


def attend(pack_items):
    queries, key_part, value_part, segment = pack_items
    scores = masked_scores(queries, key_part, segment)
    row_max = jnp.max(scores, -1, keepdims=True)
    row_total = jnp.sum(jnp.exp(scores - row_max), -1, keepdims=True)
    log_total = row_max + jnp.log(row_total)
    weights = jnp.exp(scores - log_total).astype(jnp.bfloat16)
    context = jnp.einsum("hij,jhd->ihd", weights, value_part, preferred_element_type=jnp.float32)
    return (context.astype(jnp.bfloat16), log_total)


def attend_back(pack_items):
    queries, key_part, value_part, segment, log_total, grad_context = pack_items
    probabilities = jnp.exp(masked_scores(queries, key_part, segment) - log_total)
    grad_value = jnp.einsum(
        "hij,ihd->jhd",
        probabilities.astype(jnp.bfloat16),
        grad_context,
        preferred_element_type=jnp.float32,
    ).astype(jnp.bfloat16)
    grad_probs = jnp.einsum(
        "ihd,jhd->hij", grad_context, value_part, preferred_element_type=jnp.float32
    )
    row_inner = jnp.sum(probabilities * grad_probs, -1, keepdims=True)
    grad_scores = (probabilities * (grad_probs - row_inner)).astype(jnp.bfloat16)
    grad_query = jnp.einsum(
        "hij,jhd->ihd", grad_scores, key_part, preferred_element_type=jnp.float32
    ).astype(jnp.bfloat16)
    grad_key = jnp.einsum(
        "hij,ihd->jhd", grad_scores, queries, preferred_element_type=jnp.float32
    ).astype(jnp.bfloat16)
    return (grad_query, grad_key, grad_value)


def expert_active(hidden):
    return jax.nn.gelu(hidden, approximate=True)


def contract_rows(left, right):
    return lax.dot_general(
        left, right, (((0,), (0,)), ((), ())), preferred_element_type=jnp.float32
    )


def contract_last(left, right):
    return lax.dot_general(
        left, right, (((1,), (1,)), ((), ())), preferred_element_type=jnp.float32
    )


def place_pairs(first_rows, second_rows, slot_place, slot_total):
    buffer = jnp.zeros((slot_total, first_rows.shape[-1]), jnp.bfloat16)
    return buffer.at[slot_place[:, 0]].set(first_rows).at[slot_place[:, 1]].set(second_rows)


def per_device(
    tokens,
    lengths,
    task_ids,
    routes,
    norm_gain,
    norm_bias,
    w_qkv,
    w_out,
    w_router,
    task_table,
    w_in,
    w_down,
    grad_out,
):
    row_count, model_width = tokens.shape
    owners = lax.axis_size("ep")
    capacity = max(2, 4 * row_count // owners)
    slot_total = owners * capacity
    pack_count = lengths.shape[0]
    local_width = w_qkv.shape[2]
    local_heads = local_width // HEAD_DIM
    head_scale = HEAD_DIM ** (-0.5)
    group_rows = pack_count * PACK
    pack_shape = (pack_count, PACK, local_heads, HEAD_DIM)
    tokens_f = tokens.astype(jnp.float32)
    normed_first = layer_norm(tokens_f, norm_gain[0], norm_bias[0]).astype(jnp.bfloat16)
    gathered = lax.all_gather(normed_first, "tp", axis=0, tiled=True)
    qkv_weight, out_weight = (
        lax.all_gather(w_qkv, "ep", axis=0, tiled=True),
        lax.all_gather(w_out, "ep", axis=0, tiled=True),
    )
    projected = jnp.einsum("rd,dch->rch", gathered, qkv_weight, preferred_element_type=jnp.float32)
    queries = (projected[:, 0] * head_scale).astype(jnp.bfloat16).reshape(pack_shape)
    key_part = projected[:, 1].astype(jnp.bfloat16).reshape(pack_shape)
    value_part = projected[:, 2].astype(jnp.bfloat16).reshape(pack_shape)
    segments = pack_segments(lengths)
    context, log_total = lax.map(attend, (queries, key_part, value_part, segments))
    context = context.reshape(group_rows, local_width)
    row_block = context
    attended = lax.psum_scatter(
        contract_last(row_block, out_weight), "tp", scatter_dimension=0, tiled=True
    )
    residual = tokens_f + attended
    normed_second = layer_norm(residual, norm_gain[1], norm_bias[1]).astype(jnp.bfloat16)
    expert_ids = jnp.arange(owners, dtype=jnp.int32)
    route_hot = (routes[:, :, None] == expert_ids).astype(jnp.float32)
    group_task = jnp.take_along_axis(task_ids, segments, axis=1).reshape(group_rows)
    token_task = lax.dynamic_slice_in_dim(
        group_task, lax.axis_index("tp") * row_count, row_count, 0
    )
    task_hot = (token_task[:, None] == jnp.arange(task_table.shape[0], dtype=jnp.int32)).astype(
        jnp.float32
    )
    logits = jnp.dot(normed_second, w_router, preferred_element_type=jnp.float32) + jnp.dot(
        task_hot, task_table, precision=lax.Precision.HIGHEST, preferred_element_type=jnp.float32
    )
    chosen = jnp.sum(route_hot * logits[:, None, :], -1)
    gate_values = jax.nn.softmax(chosen, axis=-1)
    pair_expert = routes.reshape(-1)
    pair_hot = (pair_expert[:, None] == expert_ids).astype(jnp.int32)
    before = jnp.cumsum(pair_hot, axis=0) - pair_hot
    slot_index = jnp.sum(before * pair_hot, -1)
    slot_place = (pair_expert * capacity + slot_index).reshape(row_count, 2)
    outgoing = place_pairs(normed_second, normed_second, slot_place, slot_total).reshape(
        owners, capacity, model_width
    )
    received = lax.all_to_all(outgoing, "ep", split_axis=0, concat_axis=0, tiled=True).reshape(
        slot_total, model_width
    )
    first_weight, second_weight = (
        lax.all_gather(w_in, "tp", axis=1, tiled=True),
        lax.all_gather(w_down, "tp", axis=1, tiled=True),
    )
    first_weight = first_weight[0]
    second_weight = second_weight[0]
    hidden = contract_last(received, first_weight)
    active = expert_active(hidden).astype(jnp.bfloat16)
    produced = jnp.dot(active, second_weight, preferred_element_type=jnp.float32).astype(
        jnp.bfloat16
    )
    returned = lax.all_to_all(
        produced.reshape(owners, capacity, model_width),
        "ep",
        split_axis=0,
        concat_axis=0,
        tiled=True,
    ).reshape(slot_total, model_width)
    pair_out = returned[slot_place].astype(jnp.float32)
    mixed_out = (residual + jnp.sum(gate_values[:, :, None] * pair_out, 1)).astype(jnp.bfloat16)
    grad_mixed = grad_out.astype(jnp.float32)
    grad_gates = jnp.sum(pair_out * grad_mixed[:, None, :], -1)
    grad_pair = (gate_values[:, :, None] * grad_mixed[:, None, :]).astype(jnp.bfloat16)
    grad_chosen = gate_values * (grad_gates - jnp.sum(gate_values * grad_gates, -1, keepdims=True))
    grad_logits = jnp.sum(route_hot * grad_chosen[:, :, None], 1)
    grad_table = lax.dot_general(
        task_hot,
        grad_logits,
        (((0,), (0,)), ((), ())),
        precision=lax.Precision.HIGHEST,
        preferred_element_type=jnp.float32,
    )
    grad_logits_low = grad_logits.astype(jnp.bfloat16)
    grad_router = contract_rows(normed_second, grad_logits_low)
    grad_normed = contract_last(grad_logits_low, w_router)
    outgoing_grad = place_pairs(grad_pair[:, 0], grad_pair[:, 1], slot_place, slot_total).reshape(
        owners, capacity, model_width
    )
    grad_produced = lax.all_to_all(
        outgoing_grad, "ep", split_axis=0, concat_axis=0, tiled=True
    ).reshape(slot_total, model_width)
    hidden_again = contract_last(received, first_weight)
    active_again, active_back = jax.vjp(expert_active, hidden_again)
    active_low = active_again.astype(jnp.bfloat16)
    grad_active = contract_last(grad_produced, second_weight)
    grad_hidden = active_back(grad_active)[0].astype(jnp.bfloat16)
    grad_second = contract_rows(active_low, grad_produced)
    grad_first = contract_rows(grad_hidden, received)
    grad_inputs = jnp.dot(grad_hidden, first_weight, preferred_element_type=jnp.float32).astype(
        jnp.bfloat16
    )
    grad_first_own, grad_second_own = (
        lax.psum_scatter(
            grad_first.astype(jnp.bfloat16), "tp", scatter_dimension=0, tiled=True
        ).astype(jnp.float32),
        lax.psum_scatter(
            grad_second.astype(jnp.bfloat16), "tp", scatter_dimension=0, tiled=True
        ).astype(jnp.float32),
    )
    grad_back = lax.all_to_all(
        grad_inputs.reshape(owners, capacity, model_width),
        "ep",
        split_axis=0,
        concat_axis=0,
        tiled=True,
    ).reshape(slot_total, model_width)
    grad_normed = grad_normed + jnp.sum(grad_back[slot_place].astype(jnp.float32), 1)
    unused_second, norm_back_second = jax.vjp(layer_norm, residual, norm_gain[1], norm_bias[1])
    grad_from_norm, grad_gain_second, grad_bias_second = norm_back_second(grad_normed)
    grad_residual = grad_mixed + grad_from_norm
    grad_attended = grad_residual.astype(jnp.bfloat16)
    grad_attended_all = lax.all_gather(grad_attended, "tp", axis=0, tiled=True)
    grad_context = jnp.dot(
        grad_attended_all, out_weight, preferred_element_type=jnp.float32
    ).astype(jnp.bfloat16)
    grad_proj = contract_rows(grad_attended_all, context)
    grad_query, grad_key, grad_value = lax.map(
        attend_back,
        (queries, key_part, value_part, segments, log_total, grad_context.reshape(pack_shape)),
    )
    grad_projected = jnp.stack(
        [
            (grad_query * head_scale).reshape(group_rows, local_width),
            grad_key.reshape(group_rows, local_width),
            grad_value.reshape(group_rows, local_width),
        ],
        axis=1,
    )
    grad_qkv = jnp.einsum(
        "rd,rch->dch", gathered, grad_projected, preferred_element_type=jnp.float32
    )
    row_block = grad_projected
    grad_normed_first = lax.psum_scatter(
        jnp.einsum("rch,dch->rd", row_block, qkv_weight, preferred_element_type=jnp.float32).astype(
            jnp.bfloat16
        ),
        "tp",
        scatter_dimension=0,
        tiled=True,
    ).astype(jnp.float32)
    unused_first, norm_back_first = jax.vjp(layer_norm, tokens_f, norm_gain[0], norm_bias[0])
    grad_from_first, grad_gain_first, grad_bias_first = norm_back_first(grad_normed_first)
    grad_tokens = (grad_residual + grad_from_first).astype(jnp.bfloat16)
    grad_qkv_own, grad_proj_own = (
        lax.psum_scatter(grad_qkv, "ep", scatter_dimension=0, tiled=True),
        lax.psum_scatter(grad_proj, "ep", scatter_dimension=0, tiled=True),
    )
    grad_gain = jnp.stack([grad_gain_first, grad_gain_second])
    grad_bias = jnp.stack([grad_bias_first, grad_bias_second])
    grad_gain, grad_bias, grad_router, grad_table = lax.psum(
        (grad_gain, grad_bias, grad_router, grad_table), ("tp", "ep")
    )
    return (
        mixed_out,
        grad_tokens,
        grad_gain,
        grad_bias,
        grad_qkv_own,
        grad_proj_own,
        grad_router,
        grad_table,
        grad_first_own.reshape(w_in.shape),
        grad_second_own.reshape(w_down.shape),
    )


def solution(mesh):
    placed = (
        P(("ep", "tp"), None),
        P("ep", None),
        P("ep", None),
        P(("ep", "tp"), None),
        P(),
        P(),
        P("ep", None, "tp"),
        P("ep", "tp"),
        P(),
        P(),
        P("ep", "tp", None),
        P("ep", "tp", None),
        P(("ep", "tp"), None),
    )
    return jax.shard_map(
        per_device,
        mesh=mesh,
        in_specs=placed,
        out_specs=(
            P(("ep", "tp"), None),
            P(("ep", "tp"), None),
            P(),
            P(),
            P("ep", None, "tp"),
            P("ep", "tp"),
            P(),
            P(),
            P("ep", "tp", None),
            P("ep", "tp", None),
        ),
        check_vma=False,
    )
```

profile of v0, /device:TPU:0, one launch (start us, length us, event | category | flops | bytes accessed | tf_op | source)
XLA Modules:
  0.0 803.2 jit_solution(12639167550335650105)
XLA Ops:
  14.9 15.7 %all_gather.20 = bf16[512,128]{1,0:T(8,128)(2,1)S(1)} all-gather(bf16[64,128]{1,0:T(8,128)(2,1)S(1)} %copy-done.59), channel_id=1, replica_groups=mesh['tp'=4,'ep'=8] {'ep'}, dimensions={0}, use_global_device_ids=true | all-gather | bytes 147456 | tf_op jit(solution)/shard_map/all_gather | solution.py:118
  30.7 14.5 %all_gather.19 = bf16[512,3,128]{2,0,1:T(8,128)(2,1)S(1)} all-gather(bf16[64,3,128]{2,0,1:T(8,128)(2,1)S(1)} %copy-done.54), channel_id=1, replica_groups=mesh['tp'=4,'ep'=8] {'ep'}, dimensions={0}, use_global_device_ids=true | all-gather | bytes 442368 | tf_op jit(solution)/shard_map/all_gather | solution.py:117
  45.2 16.3 %all-gather.5.cloned.1.call-done = bf16[3072,512]{1,0:T(8,128)(2,1)} async-done(((bf16[768,512]{1,0:T(8,128)(2,1)}), bf16[3072,512]{1,0:T(8,128)(2,1)}) %all-gather.5.cloned.1.call-update) | async-done | bytes 3145744 | tf_op jit(solution)/shard_map/all_gather | solution.py:115
  61.5 5.8 fusion.114
  76.3 23.7 %while.26 = (s32[]{:T(128)}, bf16[3,1024,2,64]{1,3,2,0:T(8,128)(2,1)S(1)}, f32[3,2,1024,1]{2,1,3,0:T(2,128)}, bf16[3,1024,2,64]{1,3,2,0:T(8,128)(2,1)}, s32[3,10...) while((s32[]{:T(128)}, ...), condition=%wide.region_7.8_spmd, body=%wide.region_4.7_spmd.sunk | while | flops 554825728 | bytes 30489176 | solution.py:125
  111.9 26.6 %gather_fusion.2 = s32[3072]{0:T(1024)S(1)} fusion(s32[3,16]{1,0:T(4,128)S(1)} %copy-done.2, s32[3072]{0:T(1024)S(1)} %reshape.401), kind=kCustom, calls=%fused_computation.2 | custom fusion | bytes 49152 | tf_op jit(solution)/shard_map/jit(take_along_axis)/gather | solution.py:135
  139.2 36.9 %reduce-scatter.7.cloned.1.call-done = f32[768,512]{1,0:T(8,128)} async-done(((f32[3072,512]{1,0:T(8,128)}), f32[768,512]{1,0:T(8,128)}) %reduce-scatter.7.cloned.1.call-update) | async-done | bytes 1572880 | tf_op jit(solution)/shard_map/reduce_scatter | solution.py:128
  181.8 8.2 %scatter_custom_fusion.2 = bf16[3072,512]{1,0:T(8,128)(2,1)} fusion(s32[768]{0:T(1024)S(1)} %get-tuple-element.202, bf16[]{:T(256)} %constant.99.clone.1, bf16[768,2,512]{2,0,1:T(8,128)(2,1)} %multiply_convert_fusion.2), kind=kCustom, calls=%fused_computation.124 | custom fusion | bytes 3932672 | tf_op jit(solution)/shard_map/scatter | solution.py:85
  190.0 10.0 %scatter_custom_fusion.3 = bf16[3072,512]{1,0:T(8,128)(2,1)} fusion(bf16[3072,512]{1,0:T(8,128)(2,1)} %scatter_custom_fusion.2, s32[768]{0:T(1024)S(1)} %get-tuple-element.201, bf16[768,2,512]{2,0,1:T(8,128)(2,1)S(1)} %copy-done.21), kind=kCustom, calls=%fused_computation.134 | custom fusion | bytes 3932160 | tf_op jit(solution)/shard_map/scatter | solution.py:85
  205.3 8.7 %scatter_custom_fusion = bf16[3072,512]{1,0:T(8,128)(2,1)} fusion(s32[768]{0:T(1024)S(1)} %get-tuple-element.202, bf16[]{:T(256)} %constant.99.clone.1, f32[768,512]{1,0:T(8,128)S(1)} %get-tuple-element.248, f32[512]{0:T(512)S(1)} %bitcast.238, f32[512]{0:T(512)S(1)} %bitcast.229, f32[768]{0:T(1024)S(1)} %fusion.104, f32[768]{0:T(1024)S(1)} %broadcast_multiply_fusion.1), kind=kCustom, calls=%fused_computation.126 | custom fusion | flops 1966080 | bytes 4730882 | tf_op jit(solution)/shard_map/scatter | solution.py:85
  214.0 10.6 %scatter_custom_fusion.1 = bf16[3072,512]{1,0:T(8,128)(2,1)} fusion(bf16[3072,512]{1,0:T(8,128)(2,1)} %scatter_custom_fusion, s32[768]{0:T(1024)S(1)} %get-tuple-element.201, f32[768,512]{1,0:T(8,128)S(1)} %get-tuple-element.248, f32[512]{0:T(512)S(1)} %bitcast.239, f32[512]{0:T(512)S(1)} %bitcast.230, f32[768]{0:T(1024)S(1)} %fusion.104, ...), kind=kCustom, calls=%fused_computation.203 | custom fusion | flops 1966080 | bytes 4730880 | tf_op jit(solution)/shard_map/scatter | solution.py:85
  224.7 51.6 %all-to-all-done.2 = bf16[8,384,512]{2,1,0:T(8,128)(2,1)} async-done(((bf16[8,384,512]{2,1,0:T(8,128)(2,1)}), bf16[8,384,512]{2,1,0:T(8,128)(2,1)}, u32[]{:S(2)}, u32[]{:S(2)}) %all-to-all-start.2) | async-done | bytes 3145760 | tf_op jit(solution)/shard_map/all_to_all | solution.py:196
  280.5 14.4 %fusion.69 = f32[3072,2048]{1,0:T(8,128)} fusion(bf16[3072,512]{1,0:T(8,128)(2,1)} %bitcast.35, bf16[1,2048,512]{2,1,0:T(8,128)(2,1)} %all-gather.9.cloned.1.call-done), kind=kOutput, calls=%fused_computation.104 | convolution fusion | flops 6442450944 | bytes 30408704 | tf_op jit(solution)/shard_map/dot_general | solution.py:78
  294.9 23.1 %all-gather.7.cloned.1.call-done = bf16[1,2048,512]{2,1,0:T(8,128)(2,1)} async-done(((bf16[1,512,512]{2,1,0:T(8,128)(2,1)}), bf16[1,2048,512]{2,1,0:T(8,128)(2,1)}) %all-gather.7.cloned.1.call-update) | async-done | bytes 2097168 | tf_op jit(solution)/shard_map/all_gather | solution.py:159
  318.0 33.3 %all-to-all-done = bf16[8,384,512]{2,1,0:T(8,128)(2,1)S(1)} async-done(((bf16[8,384,512]{2,1,0:T(8,128)(2,1)}), bf16[8,384,512]{2,1,0:T(8,128)(2,1)S(1)}, u32[]{:S(2)}, u32[]{:S(2)}) %all-to-all-start) | async-done | bytes 3145760 | tf_op jit(solution)/shard_map/all_to_all | solution.py:155
  351.4 28.9 %fusion.60 = (bf16[3072,2048]{1,0:T(8,128)(2,1)}, bf16[3072,2048]{1,0:T(8,128)(2,1)}) fusion(f32[3072,2048]{1,0:T(8,128)} %fusion.69, bf16[3072,512]{1,0:T(8,128)(2,1)S(1)} %bitcast.222, bf16[1,2048,512]{2,1,0:T(8,128)(2,1)} %all-gather.7.cloned.1.call-done), kind=kOutput, calls=%fused_computation.77 | convolution fusion | flops 6580862976 | bytes 55574528 | tf_op jit(solution)/shard_map/dot_general | solution.py:78
  380.3 10.8 %convolution_convert_fusion.3 = bf16[3072,512]{1,0:T(8,128)(2,1)} fusion(bf16[3072,2048]{1,0:T(8,128)(2,1)} %get-tuple-element.254, bf16[1,2048,512]{2,1,0:T(8,128)(2,1)S(1)} %copy-done.63), kind=kOutput, calls=%fused_computation.81 | convolution fusion | flops 6444023808 | bytes 17825792 | tf_op jit(solution)/shard_map/dot_general | solution.py:166
  395.2 13.0 %convolution_convert_fusion.2 = bf16[3072,512]{1,0:T(8,128)(2,1)} fusion(bf16[3072,2048]{1,0:T(8,128)(2,1)} %get-tuple-element.253, bf16[1,2048,512]{2,1,0:T(8,128)(2,1)} %all-gather.7.cloned.1.call-done), kind=kOutput, calls=%fused_computation.80 | convolution fusion | flops 6444023808 | bytes 17825792 | tf_op jit(solution)/shard_map/dot_general | solution.py:206
  408.2 58.4 %all-to-all-done.1 = bf16[8,384,512]{2,1,0:T(8,128)(2,1)S(1)} async-done(((bf16[8,384,512]{2,1,0:T(8,128)(2,1)}), bf16[8,384,512]{2,1,0:T(8,128)(2,1)S(1)}, u32[]{:S(2)}, u32[]{:S(2)}) %all-to-all-start.1) | async-done | bytes 3145760 | tf_op jit(solution)/shard_map/all_to_all | solution.py:169
  474.4 7.8 gather_fusion
  482.2 4.8 reshape.444
  491.8 51.6 %all-to-all-done.3 = bf16[8,384,512]{2,1,0:T(8,128)(2,1)S(1)} async-done(((bf16[8,384,512]{2,1,0:T(8,128)(2,1)}), bf16[8,384,512]{2,1,0:T(8,128)(2,1)S(1)}, u32[]{:S(2)}, u32[]{:S(2)}) %all-to-all-start.3) | async-done | bytes 3145760 | tf_op jit(solution)/shard_map/all_to_all | solution.py:217
  543.4 5.4 gather_fusion.1
  553.6 5.7 reduce_sum.240
  565.1 10.8 %convolution_convert_fusion.6 = bf16[2048,512]{1,0:T(8,128)(2,1)} fusion(bf16[3072,2048]{1,0:T(8,128)(2,1)} %get-tuple-element.253, bf16[3072,512]{1,0:T(8,128)(2,1)S(1)} %bitcast.223), kind=kOutput, calls=%fused_computation.91 | convolution fusion | flops 6443499520 | bytes 17825792 | tf_op jit(solution)/shard_map/dot_general | solution.py:72
  576.0 11.6 %convolution_convert_fusion.5 = bf16[2048,512]{1,0:T(8,128)(2,1)} fusion(bf16[3072,2048]{1,0:T(8,128)(2,1)} %get-tuple-element.254, bf16[3072,512]{1,0:T(8,128)(2,1)} %bitcast.35), kind=kOutput, calls=%fused_computation.90 | convolution fusion | flops 6443499520 | bytes 17825792 | tf_op jit(solution)/shard_map/dot_general | solution.py:72
  587.7 19.1 %all-gather.11.cloned.1.call-done = bf16[3072,512]{1,0:T(8,128)(2,1)} async-done(((bf16[768,512]{1,0:T(8,128)(2,1)}), bf16[3072,512]{1,0:T(8,128)(2,1)}) %all-gather.11.cloned.1.call-update) | async-done | bytes 3145744 | tf_op jit(solution)/shard_map/all_gather | solution.py:229
  615.3 47.3 %while.27 = (s32[]{:T(128)}, bf16[3,1024,2,64]{1,3,2,0:T(8,128)(2,1)S(1)}, bf16[3,1024,2,64]{1,3,2,0:T(8,128)(2,1)}, bf16[3,1024,2,64]{1,3,2,0:T(8,128)(2,1)}, b...) while((s32[]{:T(128)}, ...), condition=%wide.region_30.31_spmd, body=%wide.region_28.30_spmd.sunk | while | flops 1368782848 | bytes 69805168 | solution.py:234
  689.7 5.5 fusion.61
  695.5 34.7 %reduce-scatter.9.cloned.1.call-done = bf16[768,512]{1,0:T(8,128)(2,1)} async-done(((bf16[3072,512]{1,0:T(8,128)(2,1)}), bf16[768,512]{1,0:T(8,128)(2,1)}) %reduce-scatter.9.cloned.1.call-update) | async-done | bytes 786448 | tf_op jit(solution)/shard_map/reduce_scatter | solution.py:250
  734.2 40.3 %all-reduce = (f32[2,512]{1,0:T(2,128)}, f32[2,512]{1,0:T(2,128)}, f32[512,8]{0,1:T(8,128)}, f32[30,8]{0,1:T(8,128)}) all-reduce(f32[2,512]{1,0:T(2,128)S(1)} %get-tuple-element.265, f32[2,512]{1,0:T(2,128)S(1)} %get-tuple-element.266, f32[512,8]{0,1:T(8,128)S(1)} %fusion.100, ...), channel_id=1, replica_groups=mesh['tp'=4,'ep'=8] {'tp','ep'}, use_global_device_ids=true, to_apply=%region_36.37 | all-reduce | flops 6384 | bytes 51072 | tf_op jit(solution)/shard_map/psum | solution.py:267
  777.2 18.9 %reduce-scatter.11.cloned.1.call-done = f32[64,3,128]{2,0,1:T(8,128)} async-done(((f32[512,3,128]{2,0,1:T(8,128)}), f32[64,3,128]{2,0,1:T(8,128)}) %reduce-scatter.11.cloned.1.call-update) | async-done | bytes 98320 | tf_op jit(solution)/shard_map/reduce_scatter | solution.py:262
  (296 shorter events, 184.5 us)
Async XLA Ops:
  7.2 172.3 %copy-start = (bf16[512,8]{0,1:T(8,128)(2,1)S(1)}, bf16[512,8]{0,1:T(8,128)(2,1)}, u32[]{:S(2)}) copy-start(bf16[512,8]{0,1:T(8,128)(2,1)} %param.25) | copy-start | bytes 24580
  7.2 54.3 %all-gather.5.cloned.1.call-start = ((), (), s32[]{:S(2)}) async-start(), calls=%async_computation.10 | async-start | bytes 3932160 | tf_op jit(solution)/shard_map/all_gather | solution.py:115
  11.5 202.5 %copy-start.44 = (f32[1,512]{1,0:T(1,128)}, f32[1,512]{1,0:T(1,128)S(1)}, u32[]{:S(2)}) copy-start(f32[1,512]{1,0:T(1,128)S(1)} %get-tuple-element.258) | copy-start | bytes 6148
  14.7 161.4 %reduce-scatter.7.cloned.1.call-start = ((), (), s32[]{:S(2)}) async-start(), calls=%async_computation.11 | async-start | bytes 7864320 | tf_op jit(solution)/shard_map/reduce_scatter | solution.py:128
  30.6 70.6 %copy-start.31 = (bf16[512,128]{1,0:T(8,128)(2,1)}, bf16[512,128]{1,0:T(8,128)(2,1)S(1)}, u32[]{:S(2)}) copy-start(bf16[512,128]{1,0:T(8,128)(2,1)S(1)} %all_gather.20) | copy-start | bytes 393220
  111.9 64.2 %copy-start.6 = (bf16[768,512]{1,0:T(8,128)(2,1)S(1)}, bf16[768,512]{1,0:T(8,128)(2,1)}, u32[]{:S(2)}) copy-start(bf16[768,512]{1,0:T(8,128)(2,1)} %param.17) | copy-start | bytes 2359300
  138.6 41.2 %copy-start.60 = (s32[768]{0:T(1024)}, s32[768]{0:T(1024)S(1)}, u32[]{:S(2)}) copy-start(s32[768]{0:T(1024)S(1)} %dynamic-slice_select_fusion) | copy-start | bytes 9220
  177.8 36.3 %copy-start.4 = (f32[768,512]{1,0:T(8,128)}, f32[768,512]{1,0:T(8,128)S(1)}, u32[]{:S(2)}) copy-start(f32[768,512]{1,0:T(8,128)S(1)} %get-tuple-element.248) | copy-start | bytes 4718596
  177.8 36.2 %copy-start.34 = (f32[768]{0:T(1024)}, f32[768]{0:T(1024)S(1)}, u32[]{:S(2)}) copy-start(f32[768]{0:T(1024)S(1)} %broadcast_multiply_fusion.1) | copy-start | bytes 9220
  178.2 35.8 %copy-start.38 = (f32[768]{0:T(1024)}, f32[768]{0:T(1024)S(1)}, u32[]{:S(2)}) copy-start(f32[768]{0:T(1024)S(1)} %fusion.104) | copy-start | bytes 9220
  200.0 76.2 %all-to-all-start.2 = ((bf16[8,384,512]{2,1,0:T(8,128)(2,1)}), bf16[8,384,512]{2,1,0:T(8,128)(2,1)}, u32[]{:S(2)}, u32[]{:S(2)}) async-start(bf16[8,384,512]{2,1,0:T(8,128)(2,1)} %bitcast.218), calls=%async_computation.3 | async-start | bytes 6291456 | tf_op jit(solution)/shard_map/all_to_all | solution.py:196
  204.6 75.9 %all-gather.9.cloned.1.call-start = ((), (), s32[]{:S(2)}) async-start(), calls=%async_computation.13 | async-start | bytes 2621440 | tf_op jit(solution)/shard_map/all_gather | solution.py:160
  276.2 75.1 %all-to-all-start = ((bf16[8,384,512]{2,1,0:T(8,128)(2,1)}), bf16[8,384,512]{2,1,0:T(8,128)(2,1)S(1)}, u32[]{:S(2)}, u32[]{:S(2)}) async-start(bf16[8,384,512]{2,1,0:T(8,128)(2,1)} %bitcast.217), calls=%async_computation.1 | async-start | bytes 6291456 | tf_op jit(solution)/shard_map/all_to_all | solution.py:155
  279.9 38.1 %all-gather.7.cloned.1.call-start = ((), (), s32[]{:S(2)}) async-start(), calls=%async_computation.12 | async-start | bytes 2621440 | tf_op jit(solution)/shard_map/all_gather | solution.py:159
  351.4 28.9 %copy-start.25 = (bf16[8,384,512]{2,1,0:T(8,128)(2,1)}, bf16[8,384,512]{2,1,0:T(8,128)(2,1)S(1)}, u32[]{:S(2)}) copy-start(bf16[8,384,512]{2,1,0:T(8,128)(2,1)S(1)} %all-to-all-done) | copy-start | bytes 9437188
  351.4 28.9 %copy-start.63 = (bf16[1,2048,512]{2,1,0:T(8,128)(2,1)S(1)}, bf16[1,2048,512]{2,1,0:T(8,128)(2,1)}, u32[]{:S(2)}) copy-start(bf16[1,2048,512]{2,1,0:T(8,128)(2,1)} %all-gather.9.cloned.1.call-done) | copy-start | bytes 6291460
  391.1 75.5 %all-to-all-start.1 = ((bf16[8,384,512]{2,1,0:T(8,128)(2,1)}), bf16[8,384,512]{2,1,0:T(8,128)(2,1)S(1)}, u32[]{:S(2)}, u32[]{:S(2)}) async-start(bf16[8,384,512]{2,1,0:T(8,128)(2,1)} %bitcast.225), calls=%async_computation.2 | async-start | bytes 6291456 | tf_op jit(solution)/shard_map/all_to_all | solution.py:169
  468.3 75.1 %all-to-all-start.3 = ((bf16[8,384,512]{2,1,0:T(8,128)(2,1)}), bf16[8,384,512]{2,1,0:T(8,128)(2,1)S(1)}, u32[]{:S(2)}, u32[]{:S(2)}) async-start(bf16[8,384,512]{2,1,0:T(8,128)(2,1)} %bitcast.224), calls=%async_computation.4 | async-start | bytes 6291456 | tf_op jit(solution)/shard_map/all_to_all | solution.py:217
  472.0 134.8 %all-gather.11.cloned.1.call-start = ((), (), s32[]{:S(2)}) async-start(), calls=%async_computation.14 | async-start | bytes 3932160 | tf_op jit(solution)/shard_map/all_gather | solution.py:229
  564.7 113.5 %reduce-scatter.15.cloned.1.call-start = ((), (), s32[]{:S(2)}) async-start(), calls=%async_computation.18 | async-start | bytes 2621440 | tf_op jit(solution)/shard_map/reduce_scatter | solution.py:210
  575.9 30.8 %copy-start.32 = (bf16[512,128]{1,0:T(8,128)(2,1)S(1)}, bf16[512,128]{1,0:T(8,128)(2,1)}, u32[]{:S(2)}) copy-start(bf16[512,128]{1,0:T(8,128)(2,1)} %copy-done.31) | copy-start | bytes 393220
  575.9 107.3 %reduce-scatter.17.cloned.1.call-start = ((), (), s32[]{:S(2)}) async-start(), calls=%async_computation.19 | async-start | bytes 2621440 | tf_op jit(solution)/shard_map/reduce_scatter | solution.py:213
  587.6 142.6 %reduce-scatter.9.cloned.1.call-start = ((), (), s32[]{:S(2)}) async-start(), calls=%async_computation.15 | async-start | bytes 3932160 | tf_op jit(solution)/shard_map/reduce_scatter | solution.py:250
  678.2 99.0 %reduce-scatter.13.cloned.1.call-start = ((), (), s32[]{:S(2)}) async-start(), calls=%async_computation.17 | async-start | bytes 294912 | tf_op jit(solution)/shard_map/reduce_scatter | solution.py:263
  688.3 107.8 %reduce-scatter.11.cloned.1.call-start = ((), (), s32[]{:S(2)}) async-start(), calls=%async_computation.16 | async-start | bytes 884736 | tf_op jit(solution)/shard_map/reduce_scatter | solution.py:262
  689.7 40.6 %copy-start.7 = (bf16[768,512]{1,0:T(8,128)(2,1)S(1)}, bf16[768,512]{1,0:T(8,128)(2,1)}, u32[]{:S(2)}) copy-start(bf16[768,512]{1,0:T(8,128)(2,1)} %param.17) | copy-start | bytes 2359300
  689.7 40.6 %copy-start.37 = (f32[768]{0:T(1024)S(1)}, f32[768]{0:T(1024)}, u32[]{:S(2)}) copy-start(f32[768]{0:T(1024)} %copy-done.36) | copy-start | bytes 9220
  689.7 40.6 %copy-start.53 = (f32[1,512]{1,0:T(1,128)S(1)}, f32[1,512]{1,0:T(1,128)}, u32[]{:S(2)}) copy-start(f32[1,512]{1,0:T(1,128)} %copy-done.52) | copy-start | bytes 6148
  695.2 36.9 %copy-start.56 = (f32[768]{0:T(1024)S(1)}, f32[768]{0:T(1024)}, u32[]{:S(2)}) copy-start(f32[768]{0:T(1024)} %copy-done.55) | copy-start | bytes 9220
  695.2 36.9 %copy-start.47 = (f32[768]{0:T(1024)S(1)}, f32[768]{0:T(1024)}, u32[]{:S(2)}) copy-start(f32[768]{0:T(1024)} %copy-done.46) | copy-start | bytes 9220
  695.2 79.4 %copy-start.14 = (f32[768,512]{1,0:T(8,128)S(1)}, f32[768,512]{1,0:T(8,128)}, u32[]{:S(2)}) copy-start(f32[768,512]{1,0:T(8,128)} %copy-done.13) | copy-start | bytes 4718596
  730.2 44.3 %copy-start.17 = (bf16[768,512]{1,0:T(8,128)(2,1)S(1)}, bf16[768,512]{1,0:T(8,128)(2,1)}, u32[]{:S(2)}) copy-start(bf16[768,512]{1,0:T(8,128)(2,1)} %reduce-scatter.9.cloned.1.call-done) | copy-start | bytes 2359300
  (47 other events, 250.8 us)
Sparse Core Ops, SparseCore 0:
  14.8 46.6 all-gather.4
  105.9 70.2 reduce-scatter.6
  207.3 35.7 all-gather.8
  282.3 35.7 all-gather.6
  564.8 41.8 all-gather.10
  609.6 35.1 reduce-scatter.14
  648.0 35.1 reduce-scatter.16
  686.2 43.9 reduce-scatter.8
  733.1 30.4 reduce-scatter.12
  766.4 29.6 reduce-scatter.10
where the time goes:
time: 809 us; the launch traced here: 803 us
  waiting for transfers between devices  348 us (43%)
  matrix products  165 us (20%)
  local copies, waits for them, and re-layouts  109 us (13%)
  other arithmetic  78.9 us (10%)
  blocking collectives  70.5 us (9%)
  starting transfers between devices  16.4 us (2%)
  between operations  15.3 us (2%)
    all_to_all x1, waiting for transfers between devices, per_device(): lax.all_to_all(produced.reshape(owners, capacity, model_width), 'ep', spl...  58.4 us
    all_to_all x1, waiting for transfers between devices, per_device(): lax.all_to_all(grad_inputs.reshape(owners, capacity, model_width), 'ep',...  51.6 us
    all_to_all x1, waiting for transfers between devices, per_device(): lax.all_to_all(outgoing_grad, 'ep', split_axis=0, concat_axis=0, tiled=True)  51.6 us
    dot_general x4, matrix products, contract_last(): lax.dot_general(left, right, (((1,), (1,)), ((), ())), preferred_element_...  47.9 us
    psum x1, blocking collectives, per_device(): lax.psum((grad_gain, grad_bias, grad_router, grad_table), ('tp', 'ep'))  40.3 us
    reduce_scatter x1, waiting for transfers between devices, per_device(): lax.psum_scatter(contract_last(row_block, out_weight), 'tp', scatter_dime...  36.9 us
    reduce_scatter x1, waiting for transfers between devices, per_device(): lax.psum_scatter(jnp.einsum('rch,dch->rd', row_block, qkv_weight, preferr...  34.7 us
    all_to_all x1, waiting for transfers between devices, per_device(): lax.all_to_all(outgoing, 'ep', split_axis=0, concat_axis=0, tiled=True)  33.3 us
  transfers between devices with their start and end apart: 14, of which 11 were waited for; matrix products, arithmetic and copies ran while one was open for 26% of the time, Pallas kernels for 0%

commit v1 on v0

--- a/solution.py
+++ b/solution.py
@@ -1,6 +1,10 @@
+import functools
+
 import jax
 import jax.numpy as jnp
 from jax import lax
+from jax.experimental import pallas as pl
+from jax.experimental.pallas import tpu as pltpu
 from jax.sharding import PartitionSpec as P
 
 HEAD_DIM = 64
@@ -281,6 +285,608 @@
     )
 
 
+TILE = 256
+WINDOW = 3 * TILE
+PAIR = 2 * 64
+F32 = jnp.float32
+BF16 = jnp.bfloat16
+
+
+def dot_nn(left, right):
+    return lax.dot_general(left, right, (((1,), (0,)), ((), ())), preferred_element_type=F32)
+
+
+def dot_nt(left, right):
+    return lax.dot_general(left, right, (((1,), (1,)), ((), ())), preferred_element_type=F32)
+
+
+def dot_tn(left, right):
+    return lax.dot_general(left, right, (((0,), (0,)), ((), ())), preferred_element_type=F32)
+
+
+def norm_parts(rows):
+    centred = rows - jnp.mean(rows, -1, keepdims=True)
+    scale = lax.rsqrt(jnp.mean(centred * centred, -1, keepdims=True) + 1e-05)
+    return centred * scale, scale
+
+
+def norm_back(grad, gain, hat, scale):
+    weighted = grad * gain
+    return scale * (
+        weighted
+        - jnp.mean(weighted, -1, keepdims=True)
+        - hat * jnp.mean(weighted * hat, -1, keepdims=True)
+    )
+
+
+def rows_at(index, size=TILE):
+    return pl.ds(pl.multiple_of(index * size, size), size)
+
+
+def head_mask(rows, half):
+    lane = lax.broadcasted_iota(jnp.int32, (rows, PAIR), 1)
+    return (lane < 64) if half == 0 else (lane >= 64)
+
+
+def attention_forward(
+    x_ref, w_ref, seg_row, seg_col, gain_ref, bias_ref, qkv_ref, ctx_ref, res_ref, h2_ref, wo_ref, mask_ref
+):
+    own_tiles = ctx_ref.shape[0] // TILE
+    all_tiles = x_ref.shape[0] // TILE
+    pairs = w_ref.shape[0]
+
+    def project(tile, carry):
+        rows = rows_at(tile)
+        hat, _ = norm_parts(x_ref[rows, :].astype(F32))
+        normed = (hat * gain_ref[0:1, :] + bias_ref[0:1, :]).astype(BF16)
+        for pair in range(pairs):
+            out = dot_nn(normed, w_ref[pair, :, 0 : 3 * PAIR])
+            qkv_ref[pair, rows, 0:PAIR] = (out[:, 0:PAIR] * 0.125).astype(BF16)
+            qkv_ref[pair, rows, PAIR : 3 * PAIR] = out[:, PAIR:].astype(BF16)
+        return carry
+
+    lax.fori_loop(0, all_tiles, project, 0)
+    for pair in range(pairs):
+        wo_ref[:, pair * PAIR : (pair + 1) * PAIR] = w_ref[pair, :, 3 * PAIR : 4 * PAIR]
+
+    def tile_step(tile, carry):
+        own = rows_at(tile)
+        mine = rows_at(tile + 1)
+        keys = pl.ds(pl.multiple_of(tile * TILE, TILE), WINDOW)
+        mask_ref[...] = jnp.where(seg_col[mine, :] == seg_row[:, keys], 0.0, -1e30)
+
+        def pair_step(pair, inner):
+            query = qkv_ref[pair, mine, 0:PAIR]
+            key = qkv_ref[pair, keys, PAIR : 2 * PAIR]
+            value = qkv_ref[pair, keys, 2 * PAIR : 3 * PAIR]
+            parts = []
+            for half in range(2):
+                masked = jnp.where(head_mask(TILE, half), query, jnp.zeros_like(query))
+                scores = dot_nt(masked, key) + mask_ref[...]
+                expd = jnp.exp(scores - jnp.max(scores, -1, keepdims=True))
+                weights = (expd * (1.0 / jnp.sum(expd, -1, keepdims=True))).astype(BF16)
+                parts.append(dot_nn(weights, value))
+            both = jnp.where(head_mask(TILE, 0), parts[0], parts[1]).astype(BF16)
+            ctx_ref[own, pl.ds(pl.multiple_of(pair * PAIR, PAIR), PAIR)] = both
+            return inner
+
+        lax.fori_loop(0, pairs, pair_step, 0)
+        residual = x_ref[mine, :].astype(F32) + dot_nt(ctx_ref[own, :], wo_ref[...])
+        res_ref[own, :] = residual
+        hat, _ = norm_parts(residual)
+        h2_ref[own, :] = (hat * gain_ref[1:2, :] + bias_ref[1:2, :]).astype(BF16)
+        return carry
+
+    lax.fori_loop(0, own_tiles, tile_step, 0)
+
+
+def attention_backward(
+    x_ref, w_ref, seg_row, seg_col, gain_ref, bias_ref, qkv_ref, ctx_ref, gres_ref, gatt_ref,
+    gw_ref, gtok_ref, gnorm_ref,
+    mask_ref, gctx_ref, dk_ref, dv_ref, dq_ref, kt_ref, nft_ref, gnf_ref,
+):
+    own_rows = ctx_ref.shape[0]
+    own_tiles = own_rows // TILE
+    all_tiles = x_ref.shape[0] // TILE
+    pairs = w_ref.shape[0]
+    own_all = pl.ds(TILE, own_rows)
+
+    def masks(tile, carry):
+        first = jnp.clip(tile - 1, 0, all_tiles - 3)
+        keys = pl.ds(pl.multiple_of(first * TILE, TILE), WINDOW)
+        mask_ref[tile] = jnp.where(seg_col[keys, :] == seg_row[:, rows_at(tile)], 0.0, -1e30)
+        return carry
+
+    lax.fori_loop(0, all_tiles, masks, 0)
+
+    def transposes(tile, carry):
+        own = rows_at(tile)
+        hat, _ = norm_parts(x_ref[rows_at(tile + 1), :].astype(F32))
+        normed = (hat * gain_ref[0:1, :] + bias_ref[0:1, :]).astype(BF16)
+        nft_ref[0, :, own] = normed.T
+        nft_ref[1, :, own] = gatt_ref[rows_at(tile + 1), :].T
+        return carry
+
+    lax.fori_loop(0, own_tiles, transposes, 0)
+    gnf_ref[...] = jnp.zeros_like(gnf_ref)
+
+    def pair_step(pair, carry):
+        dk_ref[...] = jnp.zeros_like(dk_ref)
+        dv_ref[...] = jnp.zeros_like(dv_ref)
+
+        def prepare(tile, inner):
+            rows = rows_at(tile)
+            gctx_ref[rows, :] = dot_nn(gatt_ref[rows, :], w_ref[pair, :, 3 * PAIR : 4 * PAIR]).astype(BF16)
+            kt_ref[:, rows] = qkv_ref[pair, rows, PAIR : 2 * PAIR].T
+            return inner
+
+        lax.fori_loop(0, all_tiles, prepare, 0)
+
+        def tile_step(tile, inner):
+            rows = rows_at(tile)
+            first = jnp.clip(tile - 1, 0, all_tiles - 3)
+            keys = pl.ds(pl.multiple_of(first * TILE, TILE), WINDOW)
+            query = qkv_ref[pair, rows, 0:PAIR]
+            key = qkv_ref[pair, keys, PAIR : 2 * PAIR]
+            value = qkv_ref[pair, keys, 2 * PAIR : 3 * PAIR]
+            grad = gctx_ref[rows, :]
+            for half in range(2):
+                lanes = head_mask(TILE, half)
+                query_h = jnp.where(lanes, query, jnp.zeros_like(query))
+                grad_h = jnp.where(lanes, grad, jnp.zeros_like(grad))
+                scores = dot_nt(key, query_h) + mask_ref[tile]
+                expd = jnp.exp(scores - jnp.max(scores, 0, keepdims=True))
+                probs = expd * (1.0 / jnp.sum(expd, 0, keepdims=True))
+                grad_probs = dot_nt(value, grad_h)
+                product = probs * grad_probs
+                inner_sum = jnp.sum(product, 0, keepdims=True)
+                grad_scores = (product - probs * inner_sum).astype(BF16)
+                dv_ref[keys, :] += dot_nn(probs.astype(BF16), grad_h)
+                dk_ref[keys, :] += dot_nn(grad_scores, query_h)
+                dq_ref[half * 64 : (half + 1) * 64, rows] = dot_nn(
+                    kt_ref[half * 64 : (half + 1) * 64, keys], grad_scores
+                )
+            return inner
+
+        lax.fori_loop(0, all_tiles, tile_step, 0)
+        grad_query = (dq_ref[:, own_all].T.astype(BF16) * 0.125).astype(BF16)
+        grad_key = dk_ref[own_all, :].astype(BF16)
+        grad_value = dv_ref[own_all, :].astype(BF16)
+        grads = jnp.concatenate([grad_query, grad_key, grad_value], axis=1)
+        gw_ref[pair, :, 0 : 3 * PAIR] = dot_nn(nft_ref[0], grads).astype(gw_ref.dtype)
+        lanes = pl.ds(pl.multiple_of(pair * PAIR, PAIR), PAIR)
+        gw_ref[pair, :, 3 * PAIR : 4 * PAIR] = dot_nn(nft_ref[1], ctx_ref[:, lanes]).astype(gw_ref.dtype)
+        gnf_ref[...] += dot_nt(grads, w_ref[pair, :, 0 : 3 * PAIR])
+        return carry
+
+    lax.fori_loop(0, pairs, pair_step, 0)
+
+    def finish(tile, carry):
+        own = rows_at(tile)
+        hat, scale = norm_parts(x_ref[rows_at(tile + 1), :].astype(F32))
+        grad = gnf_ref[own, :]
+        gtok_ref[own, :] = (gres_ref[own, :] + norm_back(grad, gain_ref[0:1, :], hat, scale)).astype(BF16)
+        return (carry[0] + jnp.sum(grad * hat, 0, keepdims=True), carry[1] + jnp.sum(grad, 0, keepdims=True))
+
+    zero = jnp.zeros((1, x_ref.shape[1]), F32)
+    gain_sum, bias_sum = lax.fori_loop(0, own_tiles, finish, (zero, zero))
+    gnorm_ref[0:1, :] = gain_sum
+    gnorm_ref[1:2, :] = bias_sum
+
+
+MESH = pl.DeviceIdType.MESH
+
+
+def greet(peers):
+    barrier = pltpu.get_barrier_semaphore()
+    for peer in peers:
+        pl.semaphore_signal(barrier, inc=1, device_id=peer, device_id_type=MESH)
+    pl.semaphore_wait(barrier, len(peers))
+
+
+def send(src, dst, send_sem, recv_sem, peer):
+    copy = pltpu.make_async_remote_copy(
+        src_ref=src, dst_ref=dst, send_sem=send_sem, recv_sem=recv_sem, device_id=peer, device_id_type=MESH
+    )
+    copy.start()
+    return copy
+
+
+def gather_kernel(wp_ref, x_ref, w_ref, ext_ref, blocks, local_sem, z_ss, z_rs, t_ss, t_rs, c_ss, c_rs, h_ss, h_rs):
+    tp, ep = lax.axis_index("tp"), lax.axis_index("ep")
+    z, core = ep // 2, ep % 2
+    rows = x_ref.shape[0]
+    right, left = (tp + 1) % 4, (tp + 3) % 4
+    greet(
+        [(tp ^ k, ep) for k in (1, 2, 3)] + [(tp, ep ^ (2 * k)) for k in (1, 2, 3)] + [(tp, ep ^ 1)]
+    )
+    halo = [
+        send(x_ref.at[pl.ds(rows - TILE, TILE)], ext_ref.at[pl.ds(0, TILE)], h_ss.at[0], h_rs.at[0], (right, ep)),
+        send(x_ref.at[pl.ds(0, TILE)], ext_ref.at[pl.ds(rows + TILE, TILE)], h_ss.at[1], h_rs.at[1], (left, ep)),
+    ]
+    own = pltpu.make_async_copy(wp_ref, blocks.at[tp, core, z], local_sem.at[0])
+    own.start()
+    centre = pltpu.make_async_copy(x_ref, ext_ref.at[pl.ds(TILE, rows)], local_sem.at[1])
+    centre.start()
+    along_z = [
+        send(wp_ref, blocks.at[tp, core, z], z_ss.at[k - 1], z_rs.at[k - 1], (tp, ep ^ (2 * k)))
+        for k in (1, 2, 3)
+    ]
+    own.wait()
+    along_tp = []
+    across = []
+    for k in range(4):
+        if k > 0:
+            along_z[k - 1].wait_recv()
+        block = blocks.at[tp, core, z ^ k]
+        along_tp.append([send(block, block, t_ss.at[k, m - 1], t_rs.at[k, m - 1], (tp ^ m, ep)) for m in (1, 2, 3)])
+        across.append(send(block, block, c_ss.at[k, 0], c_rs.at[k, 0], (tp, ep ^ 1)))
+    for k in range(4):
+        for m in (1, 2, 3):
+            along_tp[k][m - 1].wait_recv()
+            block = blocks.at[tp ^ m, core, z ^ k]
+            across.append(send(block, block, c_ss.at[k, m], c_rs.at[k, m], (tp, ep ^ 1)))
+    for copy in across:
+        copy.wait()
+    for k in range(3):
+        along_z[k].wait_send()
+    for k in range(4):
+        for m in range(3):
+            along_tp[k][m].wait_send()
+    for copy in halo:
+        copy.wait()
+    centre.wait()
+    size = wp_ref.shape[0]
+    for row in range(4):
+        for which in range(2):
+            for place in range(4):
+                w_ref[row, pl.ds((2 * place + which) * size, size), :] = blocks[row, which, place]
+
+
+def gather_weights(wp, tokens):
+    size, width = wp.shape
+    rows = tokens.shape[0]
+    vmem = pl.BlockSpec(memory_space=pltpu.VMEM)
+    return pl.pallas_call(
+        gather_kernel,
+        out_shape=(
+            jax.ShapeDtypeStruct((4, 8 * size, width), BF16),
+            jax.ShapeDtypeStruct((rows + 2 * TILE, width), BF16),
+        ),
+        in_specs=[vmem, vmem],
+        out_specs=(vmem, vmem),
+        scratch_shapes=[
+            pltpu.VMEM((4, 2, 4, size, width), BF16),
+            pltpu.SemaphoreType.DMA((2,)),
+            pltpu.SemaphoreType.DMA((3,)),
+            pltpu.SemaphoreType.DMA((3,)),
+            pltpu.SemaphoreType.DMA((4, 3)),
+            pltpu.SemaphoreType.DMA((4, 3)),
+            pltpu.SemaphoreType.DMA((4, 4)),
+            pltpu.SemaphoreType.DMA((4, 4)),
+            pltpu.SemaphoreType.DMA((2,)),
+            pltpu.SemaphoreType.DMA((2,)),
+        ],
+        compiler_params=pltpu.CompilerParams(collective_id=1, has_side_effects=True, vmem_limit_bytes=32 << 20),
+        name="gather_weights",
+    )(wp, tokens)
+
+
+def reduce_kernel(
+    gw_ref, small_ref, own_ref, sum_ref,
+    got1, s1, got2, s2, got3, sm, sm2, sgot1, sgot2, sgot3,
+    a_ss, a_rs, b_ss, b_rs, c_ss, c_rs, d_ss, d_rs,
+):
+    tp, ep = lax.axis_index("tp"), lax.axis_index("ep")
+    z, core = ep // 2, ep % 2
+    greet(
+        [(tp ^ k, ep) for k in (1, 2, 3)] + [(tp, ep ^ (2 * k)) for k in (1, 2, 3)] + [(tp, ep ^ 1)]
+    )
+    first = [
+        send(gw_ref.at[tp ^ k, :, 1 - core], got1.at[tp ^ k], a_ss.at[k], a_rs.at[k], (tp, ep ^ 1))
+        for k in (1, 2, 3, 0)
+    ]
+    first_small = send(small_ref, sgot1, d_ss.at[0], d_rs.at[0], (tp, ep ^ 1))
+    second = []
+    for n, k in enumerate((1, 2, 3, 0)):
+        first[n].wait_recv()
+        row = tp ^ k
+        s1[row] = (gw_ref[row, :, core].astype(F32) + got1[row].astype(F32)).astype(BF16)
+        if k > 0:
+            second.append(send(s1.at[row], got2.at[k - 1], b_ss.at[k - 1], b_rs.at[k - 1], (row, ep)))
+    first_small.wait_recv()
+    sm[...] = small_ref[...] + sgot1[...]
+    sgot2[tp] = sm[...]
+    small_tp = [
+        send(sm, sgot2.at[tp], d_ss.at[k], d_rs.at[k], (tp ^ k, ep)) for k in (1, 2, 3)
+    ]
+    for copy in second:
+        copy.wait_recv()
+    s2[...] = (
+        s1[tp].astype(F32) + got2[0].astype(F32) + got2[1].astype(F32) + got2[2].astype(F32)
+    ).astype(BF16)
+    third = [
+        send(s2.at[z ^ k], got3.at[k - 1], c_ss.at[k - 1], c_rs.at[k - 1], (tp, ep ^ (2 * k)))
+        for k in (1, 2, 3)
+    ]
+    for copy in small_tp:
+        copy.wait_recv()
+    sm2[...] = (sgot2[0] + sgot2[1]) + (sgot2[2] + sgot2[3])
+    sgot3[z] = sm2[...]
+    small_z = [
+        send(sm2, sgot3.at[z], d_ss.at[3 + k], d_rs.at[3 + k], (tp, ep ^ (2 * k))) for k in (1, 2, 3)
+    ]
+    for copy in third:
+        copy.wait_recv()
+    own_ref[...] = (s2[z].astype(F32) + got3[0].astype(F32)) + (got3[1].astype(F32) + got3[2].astype(F32))
+    for copy in small_z:
+        copy.wait_recv()
+    sum_ref[...] = (sgot3[0] + sgot3[1]) + (sgot3[2] + sgot3[3])
+    for copy in first + second + third + [first_small] + small_tp + small_z:
+        copy.wait_send()
+
+
+def reduce_all(gw, small):
+    size, width = gw.shape[1] // 8, gw.shape[2]
+    vmem = pl.BlockSpec(memory_space=pltpu.VMEM)
+    dma = pltpu.SemaphoreType.DMA
+    return pl.pallas_call(
+        reduce_kernel,
+        out_shape=(jax.ShapeDtypeStruct((size, width), F32), jax.ShapeDtypeStruct(small.shape, F32)),
+        in_specs=[vmem, vmem],
+        out_specs=(vmem, vmem),
+        scratch_shapes=[
+            pltpu.VMEM((4, 4, size, width), BF16),
+            pltpu.VMEM((4, 4, size, width), BF16),
+            pltpu.VMEM((3, 4, size, width), BF16),
+            pltpu.VMEM((4, size, width), BF16),
+            pltpu.VMEM((3, size, width), BF16),
+            pltpu.VMEM(small.shape, F32),
+            pltpu.VMEM(small.shape, F32),
+            pltpu.VMEM(small.shape, F32),
+            pltpu.VMEM((4,) + small.shape, F32),
+            pltpu.VMEM((4,) + small.shape, F32),
+            dma((4,)),
+            dma((4,)),
+            dma((3,)),
+            dma((3,)),
+            dma((3,)),
+            dma((3,)),
+            dma((7,)),
+            dma((7,)),
+        ],
+        compiler_params=pltpu.CompilerParams(collective_id=2, has_side_effects=True, vmem_limit_bytes=32 << 20),
+        name="reduce_all",
+    )(gw.reshape(4, 4, 2, size, width), small)
+
+
+def full_spec():
+    return pl.BlockSpec(memory_space=pltpu.VMEM)
+
+
+def run_forward(ext, weights, seg_row, seg_col, gain, bias):
+    total, width = ext.shape
+    rows = total - 2 * TILE
+    pairs = weights.shape[0]
+    return pl.pallas_call(
+        attention_forward,
+        out_shape=(
+            jax.ShapeDtypeStruct((pairs, total, 3 * PAIR), BF16),
+            jax.ShapeDtypeStruct((rows, width), BF16),
+            jax.ShapeDtypeStruct((rows, width), F32),
+            jax.ShapeDtypeStruct((rows, width), BF16),
+        ),
+        in_specs=[full_spec()] * 6,
+        out_specs=(full_spec(),) * 4,
+        scratch_shapes=[pltpu.VMEM((width, width), BF16), pltpu.VMEM((TILE, WINDOW), F32)],
+        compiler_params=pltpu.CompilerParams(vmem_limit_bytes=48 << 20),
+        name="attention_forward",
+    )(ext, weights, seg_row, seg_col, gain, bias)
+
+
+def run_backward(ext, weights, seg_row, seg_col, gain, bias, qkv, ctx, gres, gatt):
+    total, width = ext.shape
+    rows = total - 2 * TILE
+    pairs = weights.shape[0]
+    return pl.pallas_call(
+        attention_backward,
+        out_shape=(
+            jax.ShapeDtypeStruct((pairs, width, 4 * PAIR), BF16),
+            jax.ShapeDtypeStruct((rows, width), BF16),
+            jax.ShapeDtypeStruct((8, width), F32),
+        ),
+        in_specs=[full_spec()] * 10,
+        out_specs=(full_spec(),) * 3,
+        scratch_shapes=[
+            pltpu.VMEM((total // TILE, WINDOW, TILE), F32),
+            pltpu.VMEM((total, PAIR), BF16),
+            pltpu.VMEM((total, PAIR), F32),
+            pltpu.VMEM((total, PAIR), F32),
+            pltpu.VMEM((PAIR, total), F32),
+            pltpu.VMEM((PAIR, total), BF16),
+            pltpu.VMEM((2, width, rows), BF16),
+            pltpu.VMEM((rows, width), F32),
+        ],
+        compiler_params=pltpu.CompilerParams(vmem_limit_bytes=56 << 20),
+        name="attention_backward",
+    )(ext, weights, seg_row, seg_col, gain, bias, qkv, ctx, gres, gatt)
+
+
+def segments_of(lengths, rows):
+    ends = jnp.cumsum(lengths.reshape(-1))
+    places = lax.axis_index("tp") * rows - TILE + jnp.arange(rows + 2 * TILE, dtype=jnp.int32)
+    segment = jnp.sum((places[:, None] >= ends[None, :]).astype(jnp.int32), -1)
+    return jnp.where(places < 0, -1, segment)
+
+
+def per_device_small(
+    tokens,
+    lengths,
+    task_ids,
+    routes,
+    norm_gain,
+    norm_bias,
+    w_qkv,
+    w_out,
+    w_router,
+    task_table,
+    w_in,
+    w_down,
+    grad_out,
+):
+    row_count, model_width = tokens.shape
+    owners = lax.axis_size("ep")
+    capacity = max(2, 4 * row_count // owners)
+    slot_total = owners * capacity
+    pack_count = lengths.shape[0]
+    local_width = w_qkv.shape[2]
+    local_heads = local_width // HEAD_DIM
+    head_scale = HEAD_DIM ** (-0.5)
+    group_rows = pack_count * PACK
+    pack_shape = (pack_count, PACK, local_heads, HEAD_DIM)
+    tokens_f = tokens.astype(jnp.float32)
+    packed = jnp.concatenate([w_qkv.reshape(w_qkv.shape[0], -1), w_out], axis=1)
+    weights, ext = gather_weights(packed, tokens)
+    segment = segments_of(lengths, row_count)
+    seg_row, seg_col = segment[None, :], segment[:, None]
+    qkv, context, residual, normed_second = run_forward(
+        ext, weights, seg_row, seg_col, norm_gain, norm_bias
+    )
+    expert_ids = jnp.arange(owners, dtype=jnp.int32)
+    route_hot = (routes[:, :, None] == expert_ids).astype(jnp.float32)
+    own_seg = segment[TILE : TILE + row_count]
+    token_task = jnp.sum(
+        jnp.where(own_seg[:, None] == jnp.arange(task_ids.size)[None, :], task_ids.reshape(1, -1), 0), -1
+    )
+    task_hot = (token_task[:, None] == jnp.arange(task_table.shape[0], dtype=jnp.int32)).astype(
+        jnp.float32
+    )
+    logits = jnp.dot(normed_second, w_router, preferred_element_type=jnp.float32) + jnp.dot(
+        task_hot, task_table, precision=lax.Precision.HIGHEST, preferred_element_type=jnp.float32
+    )
+    chosen = jnp.sum(route_hot * logits[:, None, :], -1)
+    gate_values = jax.nn.softmax(chosen, axis=-1)
+    pair_expert = routes.reshape(-1)
+    pair_hot = (pair_expert[:, None] == expert_ids).astype(jnp.int32)
+    before = jnp.cumsum(pair_hot, axis=0) - pair_hot
+    slot_index = jnp.sum(before * pair_hot, -1)
+    slot_place = (pair_expert * capacity + slot_index).reshape(row_count, 2)
+    outgoing = place_pairs(normed_second, normed_second, slot_place, slot_total).reshape(
+        owners, capacity, model_width
+    )
+    received = lax.all_to_all(outgoing, "ep", split_axis=0, concat_axis=0, tiled=True).reshape(
+        slot_total, model_width
+    )
+    first_weight, second_weight = (
+        lax.all_gather(w_in, "tp", axis=1, tiled=True),
+        lax.all_gather(w_down, "tp", axis=1, tiled=True),
+    )
+    first_weight = first_weight[0]
+    second_weight = second_weight[0]
+    hidden = contract_last(received, first_weight)
+    active = expert_active(hidden).astype(jnp.bfloat16)
+    produced = jnp.dot(active, second_weight, preferred_element_type=jnp.float32).astype(
+        jnp.bfloat16
+    )
+    returned = lax.all_to_all(
+        produced.reshape(owners, capacity, model_width),
+        "ep",
+        split_axis=0,
+        concat_axis=0,
+        tiled=True,
+    ).reshape(slot_total, model_width)
+    pair_out = returned[slot_place].astype(jnp.float32)
+    mixed_out = (residual + jnp.sum(gate_values[:, :, None] * pair_out, 1)).astype(jnp.bfloat16)
+    grad_mixed = grad_out.astype(jnp.float32)
+    grad_gates = jnp.sum(pair_out * grad_mixed[:, None, :], -1)
+    grad_pair = (gate_values[:, :, None] * grad_mixed[:, None, :]).astype(jnp.bfloat16)
+    grad_chosen = gate_values * (grad_gates - jnp.sum(gate_values * grad_gates, -1, keepdims=True))
+    grad_logits = jnp.sum(route_hot * grad_chosen[:, :, None], 1)
+    grad_table = lax.dot_general(
+        task_hot,
+        grad_logits,
+        (((0,), (0,)), ((), ())),
+        precision=lax.Precision.HIGHEST,
+        preferred_element_type=jnp.float32,
+    )
+    grad_logits_low = grad_logits.astype(jnp.bfloat16)
+    grad_router = contract_rows(normed_second, grad_logits_low)
+    grad_normed = contract_last(grad_logits_low, w_router)
+    outgoing_grad = place_pairs(grad_pair[:, 0], grad_pair[:, 1], slot_place, slot_total).reshape(
+        owners, capacity, model_width
+    )
+    grad_produced = lax.all_to_all(
+        outgoing_grad, "ep", split_axis=0, concat_axis=0, tiled=True
+    ).reshape(slot_total, model_width)
+    hidden_again = contract_last(received, first_weight)
+    active_again, active_back = jax.vjp(expert_active, hidden_again)
+    active_low = active_again.astype(jnp.bfloat16)
+    grad_active = contract_last(grad_produced, second_weight)
+    grad_hidden = active_back(grad_active)[0].astype(jnp.bfloat16)
+    grad_second = contract_rows(active_low, grad_produced)
+    grad_first = contract_rows(grad_hidden, received)
+    grad_inputs = jnp.dot(grad_hidden, first_weight, preferred_element_type=jnp.float32).astype(
+        jnp.bfloat16
+    )
+    grad_first_own, grad_second_own = (
+        lax.psum_scatter(
+            grad_first.astype(jnp.bfloat16), "tp", scatter_dimension=0, tiled=True
+        ).astype(jnp.float32),
+        lax.psum_scatter(
+            grad_second.astype(jnp.bfloat16), "tp", scatter_dimension=0, tiled=True
+        ).astype(jnp.float32),
+    )
+    grad_back = lax.all_to_all(
+        grad_inputs.reshape(owners, capacity, model_width),
+        "ep",
+        split_axis=0,
+        concat_axis=0,
+        tiled=True,
+    ).reshape(slot_total, model_width)
+    grad_normed = grad_normed + jnp.sum(grad_back[slot_place].astype(jnp.float32), 1)
+    unused_second, norm_back_second = jax.vjp(layer_norm, residual, norm_gain[1], norm_bias[1])
+    grad_from_norm, grad_gain_second, grad_bias_second = norm_back_second(grad_normed)
+    grad_residual = grad_mixed + grad_from_norm
+    grad_attended = grad_residual.astype(jnp.bfloat16)
+    ring = lax.axis_size("tp")
+    from_left = lax.ppermute(
+        grad_attended[row_count - TILE :], "tp", [(i, (i + 1) % ring) for i in range(ring)]
+    )
+    from_right = lax.ppermute(grad_attended[:TILE], "tp", [(i, (i - 1) % ring) for i in range(ring)])
+    gatt = jnp.concatenate([from_left, grad_attended, from_right], axis=0)
+    gw, grad_tokens, gnorm = run_backward(
+        ext, weights, seg_row, seg_col, norm_gain, norm_bias, qkv, context, grad_residual, gatt
+    )
+    width = model_width
+    small = jnp.concatenate(
+        [
+            gnorm[0:1], grad_gain_second[None], gnorm[1:2], grad_bias_second[None],
+            jnp.zeros((4, width), F32),
+            grad_router.T,
+            jnp.pad(grad_table.T, ((0, 0), (0, width - grad_table.shape[0]))),
+        ],
+        axis=0,
+    )
+    own, total = reduce_all(gw, small)
+    grad_qkv_own = own[:, : 3 * PAIR].reshape(w_qkv.shape)
+    grad_proj_own = own[:, 3 * PAIR :]
+    grad_gain, grad_bias = total[0:2], total[2:4]
+    grad_router = total[8:16].T
+    grad_table = total[16:24, : grad_table.shape[0]].T
+    return (
+        mixed_out,
+        grad_tokens,
+        grad_gain,
+        grad_bias,
+        grad_qkv_own,
+        grad_proj_own,
+        grad_router,
+        grad_table,
+        grad_first_own.reshape(w_in.shape),
+        grad_second_own.reshape(w_down.shape),
+    )
+
+
 def solution(mesh):
     placed = (
         P(("ep", "tp"), None),
@@ -297,8 +903,9 @@
         P("ep", "tp", None),
         P(("ep", "tp"), None),
     )
+    small = mesh.shape["tp"] == 4 and mesh.shape["ep"] == 8
     return jax.shard_map(
-        per_device,
+        per_device_small if small else per_device,
         mesh=mesh,
         in_specs=placed,
         out_specs=(

time: 809 us -> 587 us (0.73)
  waiting for transfers between devices: 348 us -> 205 us
  Pallas kernels: 0 us -> 141 us
  matrix products: 165 us -> 92.4 us
  blocking collectives: 70.5 us -> 0 us
  other arithmetic: 78.9 us -> 28.5 us
  local copies, waits for them, and re-layouts: 109 us -> 75 us
    pallas_call x0 -> x4, Pallas kernels: none -> 141 us  [the longest x1 58 us: run_backward(): pl.pallas_call(attention_backward, out_shape=(jax.ShapeDtypeStruct((pairs...]
    dot_general x30 -> x5, matrix products: 90.1 us -> 25.1 us  [the longest x1 13 us: per_device_small(): jnp.dot(grad_hidden, first_weight, preferred_element_type=jnp.float32)]
    reduce_scatter x6 -> x2, waiting for transfers between devices: 93.2 us -> 31.6 us  [the longest x1 31.6 us: per_device_small(): lax.psum_scatter(grad_second.astype(jnp.bfloat16), 'tp', scatter_dimensio...]
    all_to_all x4, waiting for transfers between devices: 195 us -> 139 us  [the longest x1 52.6 us: per_device_small(): lax.all_to_all(outgoing_grad, 'ep', split_axis=0, concat_axis=0, tiled=True)]
    psum x1 -> x0, blocking collectives: 40.3 us -> none  [per_device(): lax.psum((grad_gain, grad_bias, grad_router, grad_table), ('tp', 'ep'))]
    all_gather x4 -> x2, waiting for transfers between devices: 58.5 us -> 22.6 us  [the longest x1 22.5 us: per_device_small(): lax.all_gather(w_in, 'tp', axis=1, tiled=True)]
    all_gather x2 -> x0, blocking collectives: 30.2 us -> none  [the longest x1 15.7 us: per_device(): lax.all_gather(w_out, 'ep', axis=0, tiled=True)]
    gather x4 -> x2, local copies, waits for them, and re-layouts: 39.8 us -> 14.9 us  [the longest x1 7.77 us: per_device_small(): pair_out = returned[slot_place].astype(jnp.float32)]
  transfers between devices with their start and end apart: 14 -> 10, of which waited for: 11 -> 8; matrix products, arithmetic and copies ran while one was open for 26% -> 16% of each run, Pallas kernels for 0% -> 0%
where the time goes in v1:
time: 587 us; the launch traced here: 578 us
  waiting for transfers between devices  205 us (35%)
  Pallas kernels  141 us (24%)
  matrix products  92.4 us (16%)
  local copies, waits for them, and re-layouts  75 us (13%)
  other arithmetic  28.5 us (5%)
  starting transfers between devices  20.9 us (4%)
  between operations  14.8 us (3%)
    pallas_call x1, Pallas kernels, run_backward(): pl.pallas_call(attention_backward, out_shape=(jax.ShapeDtypeStruct((pairs...  58 us
    all_to_all x1, waiting for transfers between devices, per_device_small(): lax.all_to_all(outgoing_grad, 'ep', split_axis=0, concat_axis=0, tiled=True)  52.6 us
    all_to_all x1, waiting for transfers between devices, per_device_small(): lax.all_to_all(produced.reshape(owners, capacity, model_width), 'ep', spl...  46.9 us
    dot_general x3, matrix products, contract_last(): lax.dot_general(left, right, (((1,), (1,)), ((), ())), preferred_element_...  43.8 us
    scatter x4, local copies, waits for them, and re-layouts, place_pairs(): buffer.at[slot_place[:, 0]].set(first_rows).at[slot_place[:, 1]]  36.7 us
    all_to_all x1, waiting for transfers between devices, per_device_small(): lax.all_to_all(outgoing, 'ep', split_axis=0, concat_axis=0, tiled=True)  34 us
    pallas_call x1, Pallas kernels, gather_weights(): pl.pallas_call(gather_kernel, out_shape=(jax.ShapeDtypeStruct((4, 8 * siz...  32.1 us
    reduce_scatter x1, waiting for transfers between devices, per_device_small(): lax.psum_scatter(grad_second.astype(jnp.bfloat16), 'tp', scatter_dimensio...  31.6 us
  transfers between devices with their start and end apart: 10, of which 8 were waited for; matrix products, arithmetic and copies ran while one was open for 16% of the time, Pallas kernels for 0%

profile of v1, /device:TPU:0, one launch (start us, length us, event | category | flops | bytes accessed | tf_op | source)
XLA Modules:
  0.0 577.6 jit_solution(2850727599233138254)
XLA Ops:
  12.7 32.1 %gather_weights.1 = (bf16[4,512,512]{2,1,0:T(8,128)(2,1)S(1)}, bf16[1280,512]{1,0:T(8,128)(2,1)S(1)}) custom-call(bf16[64,512]{1,0:T(8,128)(2,1)S(1)} %pad_maximum_fusion.1.wp_ref, bf16[768,512]{1,0:T(8,128)(2,1)S(1)} %copy-done.9), custom_call_target="tpu_custom_call" | custom-call | tf_op jit(solution)/shard_map/gather_weights/pallas_call | solution.py:550
  47.5 25.2 %attention_forward.1 = (bf16[4,1280,384]{2,1,0:T(8,128)(2,1)}, bf16[768,512]{1,0:T(8,128)(2,1)S(1)}, f32[768,512]{1,0:T(8,128)S(1)}, bf16[768,512]{1,0:T(8,128)(2,1)S(1)}) custom-call(bf16[1280,512]{1,0:T(8,128)(2,1)S(1)} %get-tuple-element.21.x_ref, bf16[4,512,512]{2,1,0:T(8,128)(2,1)} %copy-done.2, s32[1,1280]{1,0:T(1,128)S(1)} %compare_select_fusion.1.seg_row, ...), custom_call_target="tpu_custom_call" | custom-call | tf_op jit(solution)/shard_map/attention_forward/pallas_call | solution.py:671
  83.4 8.4 %scatter_custom_fusion.2 = bf16[3072,512]{1,0:T(8,128)(2,1)} fusion(s32[768]{0:T(1024)S(1)} %get-tuple-element.88, bf16[]{:T(256)} %constant.16.clone.1, bf16[768,2,512]{2,0,1:T(8,128)(2,1)} %multiply_convert_fusion.1), kind=kCustom, calls=%fused_computation.35 | custom fusion | bytes 3932672 | tf_op jit(solution)/shard_map/scatter | solution.py:89
  91.8 10.2 %scatter_custom_fusion.3 = bf16[3072,512]{1,0:T(8,128)(2,1)} fusion(bf16[3072,512]{1,0:T(8,128)(2,1)} %scatter_custom_fusion.2, s32[768]{0:T(1024)S(1)} %get-tuple-element.87, bf16[768,2,512]{2,0,1:T(8,128)(2,1)} %multiply_convert_fusion.1), kind=kCustom, calls=%fused_computation.43 | custom fusion | bytes 3932160 | tf_op jit(solution)/shard_map/scatter | solution.py:89
  102.0 4.4 all-to-all-start.2
  107.2 7.8 %scatter_custom_fusion = bf16[3072,512]{1,0:T(8,128)(2,1)} fusion(s32[768]{0:T(1024)S(1)} %get-tuple-element.88, bf16[768,512]{1,0:T(8,128)(2,1)S(1)} %get-tuple-element.24, bf16[]{:T(256)} %constant.16.clone.1), kind=kCustom, calls=%fused_computation.37 | custom fusion | bytes 3145730 | tf_op jit(solution)/shard_map/scatter | solution.py:89
  115.0 10.4 %scatter_fusion = bf16[3072,512]{1,0:T(8,128)(2,1)} fusion(bf16[3072,512]{1,0:T(8,128)(2,1)} %scatter_custom_fusion, s32[768]{0:T(1024)S(1)} %get-tuple-element.87, bf16[768,512]{1,0:T(8,128)(2,1)S(1)} %get-tuple-element.24), kind=kCustom, calls=%fused_computation.3 | custom fusion | bytes 2362368 | tf_op jit(solution)/shard_map/scatter | solution.py:89
  125.3 52.6 %all-to-all-done.2 = bf16[8,384,512]{2,1,0:T(8,128)(2,1)} async-done(((bf16[8,384,512]{2,1,0:T(8,128)(2,1)}), bf16[8,384,512]{2,1,0:T(8,128)(2,1)}, u32[]{:S(2)}, u32[]{:S(2)}) %all-to-all-start.2) | async-done | bytes 3145760 | tf_op jit(solution)/shard_map/all_to_all | solution.py:818
  178.0 4.4 all-to-all-start
  183.2 14.2 %fusion.7 = f32[3072,2048]{1,0:T(8,128)} fusion(bf16[3072,512]{1,0:T(8,128)(2,1)} %bitcast.10, bf16[1,2048,512]{2,1,0:T(8,128)(2,1)} %all-gather.5.cloned.1.call-done), kind=kOutput, calls=%fused_computation.24 | convolution fusion | flops 6442450944 | bytes 30408704 | tf_op jit(solution)/shard_map/dot_general | solution.py:82
  197.4 22.5 %all-gather.3.cloned.1.call-done = bf16[1,2048,512]{2,1,0:T(8,128)(2,1)} async-done(((bf16[1,512,512]{2,1,0:T(8,128)(2,1)}), bf16[1,2048,512]{2,1,0:T(8,128)(2,1)}) %all-gather.3.cloned.1.call-update) | async-done | bytes 2097168 | tf_op jit(solution)/shard_map/all_gather | solution.py:781
  219.9 34.0 %all-to-all-done = bf16[8,384,512]{2,1,0:T(8,128)(2,1)} async-done(((bf16[8,384,512]{2,1,0:T(8,128)(2,1)}), bf16[8,384,512]{2,1,0:T(8,128)(2,1)}, u32[]{:S(2)}, u32[]{:S(2)}) %all-to-all-start) | async-done | bytes 3145760 | tf_op jit(solution)/shard_map/all_to_all | solution.py:777
  254.0 28.7 %fusion.6 = (bf16[3072,2048]{1,0:T(8,128)(2,1)}, bf16[3072,2048]{1,0:T(8,128)(2,1)}) fusion(f32[3072,2048]{1,0:T(8,128)} %fusion.7, bf16[3072,512]{1,0:T(8,128)(2,1)} %bitcast.2, bf16[1,2048,512]{2,1,0:T(8,128)(2,1)} %all-gather.3.cloned.1.call-done), kind=kOutput, calls=%fused_computation.14 | convolution fusion | flops 6580862976 | bytes 55574528 | tf_op jit(solution)/shard_map/dot_general | solution.py:82
  282.7 11.1 %convolution_convert_fusion.1 = bf16[3072,512]{1,0:T(8,128)(2,1)} fusion(bf16[3072,2048]{1,0:T(8,128)(2,1)} %get-tuple-element.96, bf16[1,2048,512]{2,1,0:T(8,128)(2,1)S(1)} %copy-done.31), kind=kOutput, calls=%fused_computation.17 | convolution fusion | flops 6444023808 | bytes 17825792 | tf_op jit(solution)/shard_map/dot_general | solution.py:788
  293.7 4.4 all-to-all-start.1
  298.2 11.6 %convolution_convert_fusion.3 = bf16[2048,512]{1,0:T(8,128)(2,1)} fusion(bf16[3072,2048]{1,0:T(8,128)(2,1)} %get-tuple-element.95, bf16[3072,512]{1,0:T(8,128)(2,1)} %bitcast.2), kind=kOutput, calls=%fused_computation.22 | convolution fusion | flops 6443499520 | bytes 17825792 | tf_op jit(solution)/shard_map/dot_general | solution.py:76
  309.9 13.0 %convolution_convert_fusion = bf16[3072,512]{1,0:T(8,128)(2,1)} fusion(bf16[3072,2048]{1,0:T(8,128)(2,1)} %get-tuple-element.95, bf16[1,2048,512]{2,1,0:T(8,128)(2,1)} %all-gather.3.cloned.1.call-done), kind=kOutput, calls=%fused_computation.16 | convolution fusion | flops 6444023808 | bytes 17825792 | tf_op jit(solution)/shard_map/dot_general | solution.py:828
  322.9 46.9 %all-to-all-done.1 = bf16[8,384,512]{2,1,0:T(8,128)(2,1)} async-done(((bf16[8,384,512]{2,1,0:T(8,128)(2,1)}), bf16[8,384,512]{2,1,0:T(8,128)(2,1)}, u32[]{:S(2)}, u32[]{:S(2)}) %all-to-all-start.1) | async-done | bytes 3145760 | tf_op jit(solution)/shard_map/all_to_all | solution.py:791
  369.7 4.5 all-to-all-start.3
  374.3 11.8 %convolution_convert_fusion.2 = bf16[2048,512]{1,0:T(8,128)(2,1)} fusion(bf16[3072,2048]{1,0:T(8,128)(2,1)} %get-tuple-element.96, bf16[3072,512]{1,0:T(8,128)(2,1)} %bitcast.10), kind=kOutput, calls=%fused_computation.21 | convolution fusion | flops 6443499520 | bytes 17825792 | tf_op jit(solution)/shard_map/dot_general | solution.py:76
  389.3 31.6 %reduce-scatter.5.cloned.1.call-done = bf16[512,512]{1,0:T(8,128)(2,1)} async-done(((bf16[2048,512]{1,0:T(8,128)(2,1)}), bf16[512,512]{1,0:T(8,128)(2,1)}) %reduce-scatter.5.cloned.1.call-update) | async-done | bytes 524304 | tf_op jit(solution)/shard_map/reduce_scatter | solution.py:835
  423.0 7.8 %gather_fusion = bf16[1536,512]{1,0:T(8,128)(2,1)} fusion(bf16[3072,512]{1,0:T(8,128)(2,1)} %bitcast.6, s32[2048]{0:T(1024)S(1)} %pad_clamp_fusion), kind=kCustom, calls=%fused_computation | custom fusion | bytes 3151872 | tf_op jit(solution)/shard_map/gather | solution.py:798
  430.8 4.9 reshape.346
  435.7 4.3 multiply_reduce_fusion
  440.1 5.6 all-to-all-done.3
  445.7 7.2 %gather_fusion.1 = bf16[1536,512]{1,0:T(8,128)(2,1)S(1)} fusion(bf16[3072,512]{1,0:T(8,128)(2,1)} %bitcast.12, s32[2048]{0:T(1024)S(1)} %pad_clamp_fusion), kind=kCustom, calls=%fused_computation.1 | custom fusion | bytes 3151872 | tf_op jit(solution)/shard_map/gather | solution.py:846
  452.9 3.5 reshape.347
  456.4 5.6 reduce_sum.178
  470.1 6.6 %collective-permute-done = bf16[256,512]{1,0:T(8,128)(2,1)S(1)} collective-permute-done((bf16[256,512]{1,0:T(8,128)(2,1)S(1)}, bf16[256,512]{1,0:T(8,128)(2,1)S(1)}, u32[]{:S(2)}, u32[]{:S(2)}) %collective-permute-start) | collective-permute-done | bytes 262176 | tf_op jit(solution)/shard_map/ppermute | solution.py:852
  476.7 3.3 collective-permute-done.1
  481.2 58.0 %attention_backward.1 = (bf16[4,512,512]{2,1,0:T(8,128)(2,1)}, bf16[768,512]{1,0:T(8,128)(2,1)}, f32[8,512]{1,0:T(8,128)}) custom-call(bf16[1280,512]{1,0:T(8,128)(2,1)} %copy-done.6, bf16[4,512,512]{2,1,0:T(8,128)(2,1)} %copy-done.2, s32[1,1280]{1,0:T(1,128)} %copy-done.10, s32[1280,1]{1,0:T(8,128)} %copy-done.5, f32[2,512]{1,0:T(2,128)} %gain_ref.3, ...), custom_call_target="tpu_custom_call" | custom-call | tf_op jit(solution)/shard_map/attention_backward/pallas_call | solution.py:691
  541.7 25.8 %reduce_all.1 = (f32[64,512]{1,0:T(8,128)S(1)}, f32[24,512]{1,0:T(8,128)S(1)}) custom-call(bf16[4,4,2,64,512]{4,3,2,1,0:T(8,128)(2,1)S(1)} %bitcast.83, f32[24,512]{1,0:T(8,128)S(1)} %concatenate.11.small_ref), custom_call_target="tpu_custom_call" | custom-call | tf_op jit(solution)/shard_map/reduce_all/pallas_call | solution.py:633
  (142 shorter events, 40.3 us)
Async XLA Ops:
  7.2 2.9 copy-start
  8.5 64.2 %copy-start.5 = (s32[1280,1]{1,0:T(8,128)}, s32[1280,1]{1,0:T(8,128)S(1)}, u32[]{:S(2)}) copy-start(s32[1280,1]{1,0:T(8,128)S(1)} %reshape_select_fusion.seg_col) | copy-start | bytes 15364
  8.6 64.2 %copy-start.10 = (s32[1,1280]{1,0:T(1,128)}, s32[1,1280]{1,0:T(1,128)S(1)}, u32[]{:S(2)}) copy-start(s32[1,1280]{1,0:T(1,128)S(1)} %compare_select_fusion.1.seg_row) | copy-start | bytes 15364
  8.6 65.0 %copy-start.27 = (bf16[512,8]{0,1:T(8,128)(2,1)S(1)}, bf16[512,8]{0,1:T(8,128)(2,1)}, u32[]{:S(2)}) copy-start(bf16[512,8]{0,1:T(8,128)(2,1)} %param.21) | copy-start | bytes 24580
  9.8 64.2 %copy-start.32 = (f32[30,8]{0,1:T(8,128)S(1)}, f32[30,8]{0,1:T(8,128)}, u32[]{:S(2)}) copy-start(f32[30,8]{0,1:T(8,128)} %param.22) | copy-start | bytes 2884
  10.0 64.4 %copy-start.21 = (s32[768,2]{0,1:T(2,128)S(1)}, s32[768,2]{0,1:T(2,128)}, u32[]{:S(2)}) copy-start(s32[768,2]{0,1:T(2,128)} %param.16) | copy-start | bytes 18436
  46.1 27.5 %copy-start.6 = (bf16[1280,512]{1,0:T(8,128)(2,1)}, bf16[1280,512]{1,0:T(8,128)(2,1)S(1)}, u32[]{:S(2)}) copy-start(bf16[1280,512]{1,0:T(8,128)(2,1)S(1)} %get-tuple-element.21.x_ref) | copy-start | bytes 3932164
  73.6 41.4 %copy-start.3 = (bf16[768,512]{1,0:T(8,128)(2,1)}, bf16[768,512]{1,0:T(8,128)(2,1)S(1)}, u32[]{:S(2)}) copy-start(bf16[768,512]{1,0:T(8,128)(2,1)S(1)} %get-tuple-element.24) | copy-start | bytes 2359300
  74.0 5.4 copy-start.29
  74.6 8.8 %copy-start.25 = (f32[768,2]{0,1:T(2,128)}, f32[768,2]{0,1:T(2,128)S(1)}, u32[]{:S(2)}) copy-start(f32[768,2]{0,1:T(2,128)S(1)} %fusion.29) | copy-start | bytes 18436
  102.0 76.0 %all-to-all-start.2 = ((bf16[8,384,512]{2,1,0:T(8,128)(2,1)}), bf16[8,384,512]{2,1,0:T(8,128)(2,1)}, u32[]{:S(2)}, u32[]{:S(2)}) async-start(bf16[8,384,512]{2,1,0:T(8,128)(2,1)} %bitcast.85), calls=%async_computation.2 | async-start | bytes 6291456 | tf_op jit(solution)/shard_map/all_to_all | solution.py:818
  106.4 76.8 %all-gather.5.cloned.1.call-start = ((), (), s32[]{:S(2)}) async-start(), calls=%async_computation.7 | async-start | bytes 2621440 | tf_op jit(solution)/shard_map/all_gather | solution.py:782
  178.0 76.0 %all-to-all-start = ((bf16[8,384,512]{2,1,0:T(8,128)(2,1)}), bf16[8,384,512]{2,1,0:T(8,128)(2,1)}, u32[]{:S(2)}, u32[]{:S(2)}) async-start(bf16[8,384,512]{2,1,0:T(8,128)(2,1)} %bitcast.84), calls=%async_computation | async-start | bytes 6291456 | tf_op jit(solution)/shard_map/all_to_all | solution.py:777
  182.4 37.5 %all-gather.3.cloned.1.call-start = ((), (), s32[]{:S(2)}) async-start(), calls=%async_computation.6 | async-start | bytes 2621440 | tf_op jit(solution)/shard_map/all_gather | solution.py:781
  254.0 28.7 %copy-start.31 = (bf16[1,2048,512]{2,1,0:T(8,128)(2,1)S(1)}, bf16[1,2048,512]{2,1,0:T(8,128)(2,1)}, u32[]{:S(2)}) copy-start(bf16[1,2048,512]{2,1,0:T(8,128)(2,1)} %all-gather.5.cloned.1.call-done) | copy-start | bytes 6291460
  293.7 76.0 %all-to-all-start.1 = ((bf16[8,384,512]{2,1,0:T(8,128)(2,1)}), bf16[8,384,512]{2,1,0:T(8,128)(2,1)}, u32[]{:S(2)}, u32[]{:S(2)}) async-start(bf16[8,384,512]{2,1,0:T(8,128)(2,1)} %bitcast.87), calls=%async_computation.1 | async-start | bytes 6291456 | tf_op jit(solution)/shard_map/all_to_all | solution.py:791
  298.2 88.9 %reduce-scatter.3.cloned.1.call-start = ((), (), s32[]{:S(2)}) async-start(), calls=%async_computation.8 | async-start | bytes 2621440 | tf_op jit(solution)/shard_map/reduce_scatter | solution.py:832
  369.7 76.0 %all-to-all-start.3 = ((bf16[8,384,512]{2,1,0:T(8,128)(2,1)}), bf16[8,384,512]{2,1,0:T(8,128)(2,1)}, u32[]{:S(2)}, u32[]{:S(2)}) async-start(bf16[8,384,512]{2,1,0:T(8,128)(2,1)} %bitcast.86), calls=%async_computation.3 | async-start | bytes 6291456 | tf_op jit(solution)/shard_map/all_to_all | solution.py:839
  374.2 11.9 %copy-start.12 = (f32[2,512]{1,0:T(2,128)S(1)}, f32[2,512]{1,0:T(2,128)}, u32[]{:S(2)}) copy-start(f32[2,512]{1,0:T(2,128)} %gain_ref.3) | copy-start | bytes 12292
  374.2 46.6 %reduce-scatter.5.cloned.1.call-start = ((), (), s32[]{:S(2)}) async-start(), calls=%async_computation.9 | async-start | bytes 2621440 | tf_op jit(solution)/shard_map/reduce_scatter | solution.py:835
  430.8 4.9 copy-start.14
  430.8 4.9 copy-start.26
  435.7 4.3 copy-start.18
  435.7 4.3 copy-start.20
  435.7 4.3 copy-start.24
  435.7 4.4 copy-start.22
  456.4 5.7 copy-start.28
  465.1 4.4 copy-start.30
  465.1 4.8 copy-start.4
  466.6 10.2 %collective-permute-start = (bf16[256,512]{1,0:T(8,128)(2,1)S(1)}, bf16[256,512]{1,0:T(8,128)(2,1)S(1)}, u32[]{:S(2)}, u32[]{:S(2)}) collective-permute-start(bf16[256,512]{1,0:T(8,128)(2,1)S(1)} %get-tuple-element.98), channel_id=1, source_target_pairs={{0,8},{8,16},{16,24},{24,0},{1,9},{9,17},{17,25},{25,1},{2,10},{10... | collective-permute-start | bytes 786440 | tf_op jit(solution)/shard_map/ppermute | solution.py:852
  467.2 12.9 %collective-permute-start.1 = (bf16[256,512]{1,0:T(8,128)(2,1)S(1)}, bf16[256,512]{1,0:T(8,128)(2,1)S(1)}, u32[]{:S(2)}, u32[]{:S(2)}) collective-permute-start(bf16[256,512]{1,0:T(8,128)(2,1)S(1)} %get-tuple-element.99), channel_id=1, source_target_pairs={{0,24},{8,0},{16,8},{24,16},{1,25},{9,1},{17,9},{25,17},{2,26},{10... | collective-permute-start | bytes 786440 | tf_op jit(solution)/shard_map/ppermute | solution.py:855
  481.2 89.3 %copy-start.1 = (bf16[64,3,128]{2,0,1:T(8,128)(2,1)S(1)}, bf16[64,3,128]{2,0,1:T(8,128)(2,1)}, u32[]{:S(2)}) copy-start(bf16[64,3,128]{2,0,1:T(8,128)(2,1)} %param.19) | copy-start | bytes 147460
  (11 other events, 17.1 us)
Sparse Core Ops, SparseCore 0:
  109.1 34.7 all-gather.4
  185.1 34.7 all-gather.2
  310.0 34.6 reduce-scatter.2
  386.2 34.5 reduce-scatter.4

commit v2 on v1

--- a/solution.py
+++ b/solution.py
@@ -329,7 +329,9 @@
 
 
 def attention_forward(
-    x_ref, w_ref, seg_row, seg_col, gain_ref, bias_ref, qkv_ref, ctx_ref, res_ref, h2_ref, wo_ref, mask_ref
+    x_ref, w_ref, seg_row, seg_col, gain_ref, bias_ref, routes_ref, router_ref, task_col, table_ref,
+    qkv_ref, ctx_ref, res_ref, h2_ref, rank_ref, gate_ref, meta_ref,
+    wo_ref, mask_ref,
 ):
     own_tiles = ctx_ref.shape[0] // TILE
     all_tiles = x_ref.shape[0] // TILE
@@ -348,6 +350,12 @@
     lax.fori_loop(0, all_tiles, project, 0)
     for pair in range(pairs):
         wo_ref[:, pair * PAIR : (pair + 1) * PAIR] = w_ref[pair, :, 3 * PAIR : 4 * PAIR]
+
+    route_ranks(routes_ref, rank_ref)
+    seg_bias = jnp.dot(
+        place_segments(task_col, table_ref), table_ref[...],
+        precision=lax.Precision.HIGHEST, preferred_element_type=F32,
+    )
 
     def tile_step(tile, carry):
         own = rows_at(tile)
@@ -374,10 +382,14 @@
         residual = x_ref[mine, :].astype(F32) + dot_nt(ctx_ref[own, :], wo_ref[...])
         res_ref[own, :] = residual
         hat, _ = norm_parts(residual)
-        h2_ref[own, :] = (hat * gain_ref[1:2, :] + bias_ref[1:2, :]).astype(BF16)
+        h2 = (hat * gain_ref[1:2, :] + bias_ref[1:2, :]).astype(BF16)
+        h2_ref[own, :] = h2
+        route_tile(tile, h2, seg_col, seg_bias, routes_ref, router_ref, gate_ref)
         return carry
 
     lax.fori_loop(0, own_tiles, tile_step, 0)
+    meta_ref[0:8, :] = rank_ref[...].T[0:8, :]
+    meta_ref[8:16, :] = gate_ref[...].T[0:8, :]
 
 
 def attention_backward(
@@ -664,7 +676,7 @@
     return pl.BlockSpec(memory_space=pltpu.VMEM)
 
 
-def run_forward(ext, weights, seg_row, seg_col, gain, bias):
+def run_forward(ext, weights, seg_row, seg_col, gain, bias, routes, router, task_col, table):
     total, width = ext.shape
     rows = total - 2 * TILE
     pairs = weights.shape[0]
@@ -675,13 +687,16 @@
             jax.ShapeDtypeStruct((rows, width), BF16),
             jax.ShapeDtypeStruct((rows, width), F32),
             jax.ShapeDtypeStruct((rows, width), BF16),
+            jax.ShapeDtypeStruct((rows, LANES), F32),
+            jax.ShapeDtypeStruct((rows, LANES), F32),
+            jax.ShapeDtypeStruct((16, rows), F32),
         ),
-        in_specs=[full_spec()] * 6,
-        out_specs=(full_spec(),) * 4,
+        in_specs=[full_spec()] * 10,
+        out_specs=(full_spec(),) * 7,
         scratch_shapes=[pltpu.VMEM((width, width), BF16), pltpu.VMEM((TILE, WINDOW), F32)],
         compiler_params=pltpu.CompilerParams(vmem_limit_bytes=48 << 20),
         name="attention_forward",
-    )(ext, weights, seg_row, seg_col, gain, bias)
+    )(ext, weights, seg_row, seg_col, gain, bias, routes, router, task_col, table)
 
 
 def run_backward(ext, weights, seg_row, seg_col, gain, bias, qkv, ctx, gres, gatt):
@@ -719,6 +734,309 @@
     return jnp.where(places < 0, -1, segment)
 
 
+LANES = 128
+
+
+def route_tile(tile, h2, seg_col, seg_bias, routes_ref, router_ref, gate_ref):
+    own = rows_at(tile)
+    places = lax.broadcasted_iota(jnp.int32, (TILE, seg_bias.shape[0]), 1)
+    picked = (seg_col[rows_at(tile + 1), :] == places).astype(F32)
+    bias = jnp.dot(picked, seg_bias, precision=lax.Precision.HIGHEST, preferred_element_type=F32)
+    logits = dot_nn(h2, router_ref[...]) + bias
+    hot = hot_tile(routes_ref, own)
+    top = jnp.max(jnp.where(hot, logits, -jnp.inf), -1, keepdims=True)
+    raised = jnp.where(hot, jnp.exp(logits - top), 0.0)
+    gate_ref[own, :] = raised / jnp.sum(raised, -1, keepdims=True)
+
+
+def hot_tile(routes_ref, rows):
+    routes = routes_ref[rows, :]
+    expert = lax.broadcasted_iota(jnp.int32, (routes.shape[0], LANES), 1)
+    return (routes[:, 0:1] == expert) | (routes[:, 1:2] == expert)
+
+
+def route_ranks(routes_ref, rank_ref):
+    rows = rank_ref.shape[0]
+    hot_all = hot_tile(routes_ref, pl.ds(0, rows)).astype(F32).astype(BF16)
+
+    def step(tile, carry):
+        own = rows_at(tile)
+        row = lax.broadcasted_iota(jnp.int32, (TILE, rows), 0) + tile * TILE
+        column = lax.broadcasted_iota(jnp.int32, (TILE, rows), 1)
+        earlier = (column < row).astype(F32).astype(BF16)
+        rank_ref[own, :] = jnp.where(hot_tile(routes_ref, own), dot_nn(earlier, hot_all), -1.0)
+        return carry
+
+    lax.fori_loop(0, rows // TILE, step, 0)
+
+
+def place_segments(task_col, table_ref):
+    task = lax.broadcasted_iota(jnp.int32, (task_col.shape[0], table_ref.shape[0]), 1)
+    hot = (task_col[...] == task).astype(F32)
+    return hot
+
+
+def gelu_both(hidden):
+    square = hidden * hidden
+    factor = 0.7978845608028654
+    slope = factor * 0.044715
+    tanh = jnp.tanh(hidden * (factor + slope * square))
+    half = 0.5 + 0.5 * tanh
+    active = hidden * half
+    inner = factor + (3.0 * slope) * square
+    return active, half + active * ((1.0 - tanh) * inner)
+
+
+def expert_kernel(
+    x_ref, g_ref, meta_ref, w1_ref, w2_ref,
+    gw1_ref, gw2_ref, ret_g, ret_p, ret_s,
+    xall, gall, mall, w1t, w2t, acc1, acc2, xs_ref, gp_ref, prod_ref, back_ref, put_g, put_p, put_s,
+    in_ss, in_rs, g_ss, g_rs, p_ss, p_rs, s_ss, s_rs,
+):
+    tp, ep = lax.axis_index("tp"), lax.axis_index("ep")
+    peers = [(tp, ep ^ m) for m in (1, 2, 3)]
+    greet(peers)
+    arrive = {}
+    for m in (2, 3, 1):
+        arrive[m] = [
+            send(src, dst.at[m], in_ss.at[m - 1, n], in_rs.at[m - 1, n], (tp, ep ^ m))
+            for n, (src, dst) in enumerate(((meta_ref, mall), (x_ref, xall), (g_ref, gall)))
+        ]
+    mall[0] = meta_ref[...]
+    xall[0] = x_ref[...]
+    gall[0] = g_ref[...]
+    put_s[...] = jnp.zeros_like(put_s)
+    capacity = ret_g.shape[-1]
+    rows, width = x_ref.shape
+    hidden_rows = w1_ref.shape[1]
+    chunk = 512
+    gone = []
+    waited = set()
+    for q, sides in ((0, (0, 1)), (1, (1, 0))):
+        expert = ep ^ (4 * q)
+        for start in range(0, hidden_rows, chunk):
+            w1t[:, start : start + chunk] = w1_ref[q, start : start + chunk, :].T
+            w2t[:, start : start + chunk] = w2_ref[q, start : start + chunk, :].T
+        acc1[...] = jnp.zeros_like(acc1)
+        acc2[...] = jnp.zeros_like(acc2)
+        for side in sides:
+            gates = []
+            for part in range(2):
+                m = 2 * side + part
+                if m > 0 and m not in waited:
+                    waited.add(m)
+                    for copy in arrive[m]:
+                        copy.wait_recv()
+                slot = lax.broadcasted_iota(jnp.int32, (capacity, rows), 0).astype(F32)
+                match = slot == mall[m, pl.ds(expert, 1), :]
+                hot = match.astype(F32).astype(BF16)
+                gate = jnp.sum(jnp.where(match, mall[m, pl.ds(expert + 8, 1), :], 0.0), -1, keepdims=True)
+                gates.append(gate)
+                span = slice(part * capacity, (part + 1) * capacity)
+                xs_ref[span, :] = dot_nn(hot, xall[m]).astype(BF16)
+                picked = dot_nn(hot, gall[m])
+                gp_ref[span, :] = (picked * gate).astype(BF16)
+                back_ref[:, span] = picked.T
+            gate_row = jnp.concatenate(
+                [jnp.broadcast_to(gate, (capacity, LANES)).T[0:1, :] for gate in gates], axis=1
+            )
+            prod_ref[...] = jnp.zeros_like(prod_ref)
+
+            def step(n, carry, q=q):
+                at = pl.ds(pl.multiple_of(n * chunk, chunk), chunk)
+                xs = xs_ref[...]
+                gp = gp_ref[...]
+                hidden = dot_nt(w1_ref[q, at, :], xs)
+                grad_active = dot_nt(w2_ref[q, at, :], gp)
+                active, slope = gelu_both(hidden)
+                active = active.astype(BF16)
+                grad_hidden = (grad_active * slope).astype(BF16)
+                acc1[at, :] += dot_nn(grad_hidden, xs)
+                acc2[at, :] += dot_nn(active, gp)
+                prod_ref[0] += dot_nn(w2t[:, at], active)
+                prod_ref[1] += dot_nn(w1t[:, at], grad_hidden)
+                return carry
+
+            lax.fori_loop(0, hidden_rows // chunk, step, 0)
+            produced = prod_ref[0].astype(BF16).astype(F32)
+            grad_gate = jnp.sum(back_ref[...] * produced, 0, keepdims=True)
+            gated = (produced * gate_row).astype(BF16)
+            grad_copy = prod_ref[1].astype(BF16)
+            for part in range(2):
+                m = 2 * side + part
+                span = slice(part * capacity, (part + 1) * capacity)
+                if m == 0:
+                    ret_g[0, q] = grad_copy[:, span]
+                    ret_p[0, q] = gated[:, span]
+                    put_s[0, q : q + 1, :] = grad_gate[:, span]
+                else:
+                    put_g[m - 1, q] = grad_copy[:, span]
+                    put_p[m - 1, q] = gated[:, span]
+                    put_s[m, q : q + 1, :] = grad_gate[:, span]
+                    peer = (tp, ep ^ m)
+                    at = (m - 1, q)
+                    gone.append(send(put_g.at[m - 1, q], ret_g.at[m, q], g_ss.at[at], g_rs.at[at], peer))
+                    gone.append(send(put_p.at[m - 1, q], ret_p.at[m, q], p_ss.at[at], p_rs.at[at], peer))
+                    if q == 1:
+                        gone.append(send(put_s.at[m], ret_s.at[m], s_ss.at[m - 1], s_rs.at[m - 1], peer))
+        gw1_ref[q] = acc1[...].astype(BF16)
+        gw2_ref[q] = acc2[...].astype(BF16)
+    ret_s[0] = put_s[0]
+    for copy in gone:
+        copy.wait()
+    for m in (1, 2, 3):
+        for copy in arrive[m]:
+            copy.wait_send()
+
+
+def run_experts(x, g, meta, w1, w2, capacity):
+    rows, width = x.shape
+    hidden_rows = w1.shape[1]
+    vmem = pl.BlockSpec(memory_space=pltpu.VMEM)
+    dma = pltpu.SemaphoreType.DMA
+    back = jax.ShapeDtypeStruct((4, 2, width, capacity), BF16)
+    return pl.pallas_call(
+        expert_kernel,
+        out_shape=(
+            jax.ShapeDtypeStruct(w1.shape, BF16),
+            jax.ShapeDtypeStruct(w2.shape, BF16),
+            back,
+            back,
+            jax.ShapeDtypeStruct((4, 8, capacity), F32),
+        ),
+        in_specs=[vmem] * 5,
+        out_specs=(vmem,) * 5,
+        scratch_shapes=[
+            pltpu.VMEM((4, rows, width), BF16),
+            pltpu.VMEM((4, rows, width), BF16),
+            pltpu.VMEM((4,) + meta.shape, F32),
+            pltpu.VMEM((width, hidden_rows), BF16),
+            pltpu.VMEM((width, hidden_rows), BF16),
+            pltpu.VMEM((hidden_rows, width), F32),
+            pltpu.VMEM((hidden_rows, width), F32),
+            pltpu.VMEM((2 * capacity, width), BF16),
+            pltpu.VMEM((2 * capacity, width), BF16),
+            pltpu.VMEM((2, width, 2 * capacity), F32),
+            pltpu.VMEM((width, 2 * capacity), F32),
+            pltpu.VMEM((3, 2, width, capacity), BF16),
+            pltpu.VMEM((3, 2, width, capacity), BF16),
+            pltpu.VMEM((4, 8, capacity), F32),
+            dma((3, 3)),
+            dma((3, 3)),
+            dma((3, 2)),
+            dma((3, 2)),
+            dma((3, 2)),
+            dma((3, 2)),
+            dma((3,)),
+            dma((3,)),
+        ],
+        compiler_params=pltpu.CompilerParams(collective_id=3, has_side_effects=True, vmem_limit_bytes=60 << 20),
+        name="experts",
+    )(x, g, meta, w1, w2)
+
+
+def combine_kernel(
+    ret_g, ret_p, ret_s, rank_ref, gate_ref, res_ref, h2_ref, g_ref, gain_ref, router_ref, seg_col, task_col,
+    table_ref,
+    mixed_ref, gres_ref, gatt_ref, sums_ref, groute_ref, gtable_ref,
+):
+    ep = lax.axis_index("ep")
+    rows, width = res_ref.shape
+    capacity = ret_g.shape[-1]
+    groute_ref[...] = jnp.zeros_like(groute_ref)
+    lane = lax.broadcasted_iota(jnp.int32, (TILE, LANES), 1)
+    slot = lax.broadcasted_iota(jnp.int32, (TILE, capacity), 1).astype(F32)
+
+    def step(tile, carry):
+        own = rows_at(tile)
+        rank = rank_ref[own, :]
+        gate = gate_ref[own, :]
+        grad_copy = jnp.zeros((TILE, width), F32)
+        mixed = jnp.zeros((TILE, width), F32)
+        grad_gates = jnp.zeros((TILE, LANES), F32)
+        for m in range(4):
+            for q in range(2):
+                expert = ep ^ m ^ (4 * q)
+                here = lane == expert
+                column = jnp.sum(jnp.where(here, rank, 0.0), -1, keepdims=True)
+                match = slot == column
+                hot = match.astype(F32).astype(BF16)
+                grad_copy += dot_nt(hot, ret_g[m, q])
+                mixed += dot_nt(hot, ret_p[m, q])
+                own_gate = jnp.sum(jnp.where(match, ret_s[m, q : q + 1, :], 0.0), -1, keepdims=True)
+                grad_gates += jnp.where(here, own_gate, 0.0)
+        residual = res_ref[own, :]
+        mixed_ref[own, :] = (residual + mixed).astype(BF16)
+        grad_logits = gate * (grad_gates - jnp.sum(gate * grad_gates, -1, keepdims=True))
+        low = grad_logits.astype(BF16)
+        groute_ref[...] += dot_tn(low, h2_ref[own, :])
+        grad_normed = dot_nt(low, router_ref[...]) + grad_copy
+        places = lax.broadcasted_iota(jnp.int32, (TILE, task_col.shape[0]), 1)
+        picked = (seg_col[rows_at(tile + 1), :] == places).astype(F32)
+        by_segment = lax.dot_general(
+            picked, grad_logits, (((0,), (0,)), ((), ())), precision=lax.Precision.HIGHEST, preferred_element_type=F32
+        )
+        hat, scale = norm_parts(residual)
+        grad_residual = g_ref[own, :].astype(F32) + norm_back(grad_normed, gain_ref[1:2, :], hat, scale)
+        gres_ref[own, :] = grad_residual
+        gatt_ref[own, :] = grad_residual.astype(BF16)
+        return (
+            carry[0] + jnp.sum(grad_normed * hat, 0, keepdims=True),
+            carry[1] + jnp.sum(grad_normed, 0, keepdims=True),
+            carry[2] + by_segment,
+        )
+
+    zero = jnp.zeros((1, width), F32)
+    gain_sum, bias_sum, by_segment = lax.fori_loop(
+        0, rows // TILE, step, (zero, zero, jnp.zeros((task_col.shape[0], LANES), F32))
+    )
+    sums_ref[0:1, :] = gain_sum
+    sums_ref[1:2, :] = bias_sum
+    gtable_ref[...] = lax.dot_general(
+        place_segments(task_col, table_ref), by_segment, (((0,), (0,)), ((), ())),
+        precision=lax.Precision.HIGHEST, preferred_element_type=F32,
+    )
+
+
+def run_combine(ret_g, ret_p, ret_s, rank, gate, residual, h2, g, gain, router, seg_col, task_col, table):
+    rows, width = residual.shape
+    return pl.pallas_call(
+        combine_kernel,
+        out_shape=(
+            jax.ShapeDtypeStruct((rows, width), BF16),
+            jax.ShapeDtypeStruct((rows, width), F32),
+            jax.ShapeDtypeStruct((rows, width), BF16),
+            jax.ShapeDtypeStruct((8, width), F32),
+            jax.ShapeDtypeStruct((LANES, width), F32),
+            jax.ShapeDtypeStruct((table.shape[0], LANES), F32),
+        ),
+        in_specs=[full_spec()] * 13,
+        out_specs=(full_spec(),) * 6,
+        compiler_params=pltpu.CompilerParams(vmem_limit_bytes=56 << 20),
+        name="combine",
+    )(ret_g, ret_p, ret_s, rank, gate, residual, h2, g, gain, router, seg_col, task_col, table)
+
+
+def expert_weights(w_in, w_down):
+    width = lax.axis_size("ep")
+    swap = [(i, i ^ 4) for i in range(width)]
+    both = []
+    for weight in (w_in, w_down):
+        mirror = lax.ppermute(weight, "ep", swap)
+        own = lax.all_gather(weight, "tp", axis=1, tiled=True)
+        other = lax.all_gather(mirror, "tp", axis=1, tiled=True)
+        both.append(jnp.concatenate([own, other], axis=0))
+    return both
+
+
+def expert_grads(grad):
+    width = lax.axis_size("ep")
+    swap = [(i, i ^ 4) for i in range(width)]
+    own = lax.psum_scatter(grad[0], "tp", scatter_dimension=0, tiled=True)
+    other = lax.ppermute(lax.psum_scatter(grad[1], "tp", scatter_dimension=0, tiled=True), "ep", swap)
+    return (own.astype(F32) + other.astype(F32))[None]
+
+
 def per_device_small(
     tokens,
     lengths,
@@ -734,156 +1052,55 @@
     w_down,
     grad_out,
 ):
-    row_count, model_width = tokens.shape
+    row_count, width = tokens.shape
     owners = lax.axis_size("ep")
     capacity = max(2, 4 * row_count // owners)
-    slot_total = owners * capacity
-    pack_count = lengths.shape[0]
-    local_width = w_qkv.shape[2]
-    local_heads = local_width // HEAD_DIM
-    head_scale = HEAD_DIM ** (-0.5)
-    group_rows = pack_count * PACK
-    pack_shape = (pack_count, PACK, local_heads, HEAD_DIM)
-    tokens_f = tokens.astype(jnp.float32)
+    tasks = task_table.shape[0]
     packed = jnp.concatenate([w_qkv.reshape(w_qkv.shape[0], -1), w_out], axis=1)
     weights, ext = gather_weights(packed, tokens)
+    w1, w2 = expert_weights(w_in, w_down)
     segment = segments_of(lengths, row_count)
     seg_row, seg_col = segment[None, :], segment[:, None]
-    qkv, context, residual, normed_second = run_forward(
-        ext, weights, seg_row, seg_col, norm_gain, norm_bias
-    )
-    expert_ids = jnp.arange(owners, dtype=jnp.int32)
-    route_hot = (routes[:, :, None] == expert_ids).astype(jnp.float32)
-    own_seg = segment[TILE : TILE + row_count]
-    token_task = jnp.sum(
-        jnp.where(own_seg[:, None] == jnp.arange(task_ids.size)[None, :], task_ids.reshape(1, -1), 0), -1
-    )
-    task_hot = (token_task[:, None] == jnp.arange(task_table.shape[0], dtype=jnp.int32)).astype(
-        jnp.float32
-    )
-    logits = jnp.dot(normed_second, w_router, preferred_element_type=jnp.float32) + jnp.dot(
-        task_hot, task_table, precision=lax.Precision.HIGHEST, preferred_element_type=jnp.float32
-    )
-    chosen = jnp.sum(route_hot * logits[:, None, :], -1)
-    gate_values = jax.nn.softmax(chosen, axis=-1)
-    pair_expert = routes.reshape(-1)
-    pair_hot = (pair_expert[:, None] == expert_ids).astype(jnp.int32)
-    before = jnp.cumsum(pair_hot, axis=0) - pair_hot
-    slot_index = jnp.sum(before * pair_hot, -1)
-    slot_place = (pair_expert * capacity + slot_index).reshape(row_count, 2)
-    outgoing = place_pairs(normed_second, normed_second, slot_place, slot_total).reshape(
-        owners, capacity, model_width
-    )
-    received = lax.all_to_all(outgoing, "ep", split_axis=0, concat_axis=0, tiled=True).reshape(
-        slot_total, model_width
-    )
-    first_weight, second_weight = (
-        lax.all_gather(w_in, "tp", axis=1, tiled=True),
-        lax.all_gather(w_down, "tp", axis=1, tiled=True),
-    )
-    first_weight = first_weight[0]
-    second_weight = second_weight[0]
-    hidden = contract_last(received, first_weight)
-    active = expert_active(hidden).astype(jnp.bfloat16)
-    produced = jnp.dot(active, second_weight, preferred_element_type=jnp.float32).astype(
-        jnp.bfloat16
-    )
-    returned = lax.all_to_all(
-        produced.reshape(owners, capacity, model_width),
-        "ep",
-        split_axis=0,
-        concat_axis=0,
-        tiled=True,
-    ).reshape(slot_total, model_width)
-    pair_out = returned[slot_place].astype(jnp.float32)
-    mixed_out = (residual + jnp.sum(gate_values[:, :, None] * pair_out, 1)).astype(jnp.bfloat16)
-    grad_mixed = grad_out.astype(jnp.float32)
-    grad_gates = jnp.sum(pair_out * grad_mixed[:, None, :], -1)
-    grad_pair = (gate_values[:, :, None] * grad_mixed[:, None, :]).astype(jnp.bfloat16)
-    grad_chosen = gate_values * (grad_gates - jnp.sum(gate_values * grad_gates, -1, keepdims=True))
-    grad_logits = jnp.sum(route_hot * grad_chosen[:, :, None], 1)
-    grad_table = lax.dot_general(
-        task_hot,
-        grad_logits,
-        (((0,), (0,)), ((), ())),
-        precision=lax.Precision.HIGHEST,
-        preferred_element_type=jnp.float32,
-    )
-    grad_logits_low = grad_logits.astype(jnp.bfloat16)
-    grad_router = contract_rows(normed_second, grad_logits_low)
-    grad_normed = contract_last(grad_logits_low, w_router)
-    outgoing_grad = place_pairs(grad_pair[:, 0], grad_pair[:, 1], slot_place, slot_total).reshape(
-        owners, capacity, model_width
-    )
-    grad_produced = lax.all_to_all(
-        outgoing_grad, "ep", split_axis=0, concat_axis=0, tiled=True
-    ).reshape(slot_total, model_width)
-    hidden_again = contract_last(received, first_weight)
-    active_again, active_back = jax.vjp(expert_active, hidden_again)
-    active_low = active_again.astype(jnp.bfloat16)
-    grad_active = contract_last(grad_produced, second_weight)
-    grad_hidden = active_back(grad_active)[0].astype(jnp.bfloat16)
-    grad_second = contract_rows(active_low, grad_produced)
-    grad_first = contract_rows(grad_hidden, received)
-    grad_inputs = jnp.dot(grad_hidden, first_weight, preferred_element_type=jnp.float32).astype(
-        jnp.bfloat16
-    )
-    grad_first_own, grad_second_own = (
-        lax.psum_scatter(
-            grad_first.astype(jnp.bfloat16), "tp", scatter_dimension=0, tiled=True
-        ).astype(jnp.float32),
-        lax.psum_scatter(
-            grad_second.astype(jnp.bfloat16), "tp", scatter_dimension=0, tiled=True
-        ).astype(jnp.float32),
-    )
-    grad_back = lax.all_to_all(
-        grad_inputs.reshape(owners, capacity, model_width),
-        "ep",
-        split_axis=0,
-        concat_axis=0,
-        tiled=True,
-    ).reshape(slot_total, model_width)
-    grad_normed = grad_normed + jnp.sum(grad_back[slot_place].astype(jnp.float32), 1)
-    unused_second, norm_back_second = jax.vjp(layer_norm, residual, norm_gain[1], norm_bias[1])
-    grad_from_norm, grad_gain_second, grad_bias_second = norm_back_second(grad_normed)
-    grad_residual = grad_mixed + grad_from_norm
-    grad_attended = grad_residual.astype(jnp.bfloat16)
+    task_col = task_ids.reshape(-1, 1)
+    router = jnp.pad(w_router, ((0, 0), (0, LANES - owners)))
+    table = jnp.pad(task_table, ((0, 0), (0, LANES - owners)))
+    qkv, context, residual, normed_second, rank, gate, meta = run_forward(
+        ext, weights, seg_row, seg_col, norm_gain, norm_bias, routes, router, task_col, table
+    )
+    gw1, gw2, ret_g, ret_p, ret_s = run_experts(normed_second, grad_out, meta, w1, w2, capacity)
+    grad_in, grad_down = expert_grads(gw1), expert_grads(gw2)
+    mixed_out, gres, gatt, sums, grad_router, grad_table = run_combine(
+        ret_g, ret_p, ret_s, rank, gate, residual, normed_second, grad_out, norm_gain, router, seg_col,
+        task_col, table,
+    )
     ring = lax.axis_size("tp")
-    from_left = lax.ppermute(
-        grad_attended[row_count - TILE :], "tp", [(i, (i + 1) % ring) for i in range(ring)]
-    )
-    from_right = lax.ppermute(grad_attended[:TILE], "tp", [(i, (i - 1) % ring) for i in range(ring)])
-    gatt = jnp.concatenate([from_left, grad_attended, from_right], axis=0)
+    from_left = lax.ppermute(gatt[row_count - TILE :], "tp", [(i, (i + 1) % ring) for i in range(ring)])
+    from_right = lax.ppermute(gatt[:TILE], "tp", [(i, (i - 1) % ring) for i in range(ring)])
+    gatt_ext = jnp.concatenate([from_left, gatt, from_right], axis=0)
     gw, grad_tokens, gnorm = run_backward(
-        ext, weights, seg_row, seg_col, norm_gain, norm_bias, qkv, context, grad_residual, gatt
-    )
-    width = model_width
+        ext, weights, seg_row, seg_col, norm_gain, norm_bias, qkv, context, gres, gatt_ext
+    )
     small = jnp.concatenate(
         [
-            gnorm[0:1], grad_gain_second[None], gnorm[1:2], grad_bias_second[None],
+            gnorm[0:1], sums[0:1], gnorm[1:2], sums[1:2],
             jnp.zeros((4, width), F32),
-            grad_router.T,
-            jnp.pad(grad_table.T, ((0, 0), (0, width - grad_table.shape[0]))),
+            grad_router[:owners],
+            jnp.pad(grad_table[:, :owners].T, ((0, 0), (0, width - tasks))),
         ],
         axis=0,
     )
     own, total = reduce_all(gw, small)
-    grad_qkv_own = own[:, : 3 * PAIR].reshape(w_qkv.shape)
-    grad_proj_own = own[:, 3 * PAIR :]
-    grad_gain, grad_bias = total[0:2], total[2:4]
-    grad_router = total[8:16].T
-    grad_table = total[16:24, : grad_table.shape[0]].T
     return (
         mixed_out,
         grad_tokens,
-        grad_gain,
-        grad_bias,
-        grad_qkv_own,
-        grad_proj_own,
-        grad_router,
-        grad_table,
-        grad_first_own.reshape(w_in.shape),
-        grad_second_own.reshape(w_down.shape),
+        total[0:2],
+        total[2:4],
+        own[:, : 3 * PAIR].reshape(w_qkv.shape),
+        own[:, 3 * PAIR :],
+        total[8:16].T,
+        total[16:24, :tasks].T,
+        grad_in,
+        grad_down,
     )
 
 

time: 587 us -> 553 us (0.942)
  Pallas kernels: 141 us -> 338 us
  matrix products: 92.4 us -> 0 us
  waiting for transfers between devices: 205 us -> 139 us
  local copies, waits for them, and re-layouts: 75 us -> 25.4 us
  other arithmetic: 28.5 us -> 16.4 us
  starting transfers between devices: 20.9 us -> 10.4 us
    pallas_call x0 -> x2, Pallas kernels: none -> 179 us  [the longest x1 165 us: run_experts(): pl.pallas_call(expert_kernel, out_shape=(jax.ShapeDtypeStruct(w1.shape, B...]
    all_to_all x4 -> x0, waiting for transfers between devices: 139 us -> none  [the longest x1 52.6 us: per_device_small(): lax.all_to_all(outgoing_grad, 'ep', split_axis=0, concat_axis=0, tiled=True)]
    ppermute x2 -> x6, waiting for transfers between devices: 9.91 us -> 106 us  [the longest x2 48.8 us: expert_weights(): mirror = lax.ppermute(weight, 'ep', swap)]
    dot_general x11 -> x0, matrix products: 92.4 us -> none  [the longest x3 43.8 us: contract_last(): lax.dot_general(left, right, (((1,), (1,)), ((), ())), preferred_element_...]
    scatter x4 -> x0, local copies, waits for them, and re-layouts: 36.7 us -> none  [place_pairs(): buffer.at[slot_place[:, 0]].set(first_rows).at[slot_place[:, 1]]]
    reduce_scatter x2 -> x4, waiting for transfers between devices: 31.6 us -> 0.01 us  [the longest x2 0.01 us: expert_grads(): lax.psum_scatter(grad[1], 'tp', scatter_dimension=0, tiled=True)]
    all_to_all x4 -> x0, starting transfers between devices: 17.8 us -> none  [the longest x1 4.46 us: per_device_small(): lax.all_to_all(grad_inputs.reshape(owners, capacity, model_width), 'ep',...]
    gather x2 -> x0, local copies, waits for them, and re-layouts: 14.9 us -> none  [the longest x1 7.77 us: per_device_small(): pair_out = returned[slot_place].astype(jnp.float32)]
  transfers between devices with their start and end apart: 10 -> 14, of which waited for: 8 -> 7; matrix products, arithmetic and copies ran while one was open for 16% -> 4% of each run, Pallas kernels for 0% -> 32%
where the time goes in v2:
time: 553 us; the launch traced here: 544 us
  Pallas kernels  338 us (61%)
  waiting for transfers between devices  139 us (25%)
  local copies, waits for them, and re-layouts  25.4 us (5%)
  other arithmetic  16.4 us (3%)
  between operations  15 us (3%)
  starting transfers between devices  10.4 us (2%)
    pallas_call x1, Pallas kernels, run_experts(): pl.pallas_call(expert_kernel, out_shape=(jax.ShapeDtypeStruct(w1.shape, B...  165 us
    pallas_call x1, Pallas kernels, run_backward(): pl.pallas_call(attention_backward, out_shape=(jax.ShapeDtypeStruct((pairs...  58.2 us
    ppermute x2, waiting for transfers between devices, expert_weights(): mirror = lax.ppermute(weight, 'ep', swap)  48.8 us
    ppermute x2, waiting for transfers between devices, expert_grads(): lax.ppermute(lax.psum_scatter(grad[1], 'tp', scatter_dimension=0, tiled=T...  41.9 us
    pallas_call x1, Pallas kernels, gather_weights(): pl.pallas_call(gather_kernel, out_shape=(jax.ShapeDtypeStruct((4, 8 * siz...  39.5 us
    pallas_call x1, Pallas kernels, reduce_all(): pl.pallas_call(reduce_kernel, out_shape=(jax.ShapeDtypeStruct((size, widt...  33.2 us
    all_gather x2, waiting for transfers between devices, expert_weights(): other = lax.all_gather(mirror, 'tp', axis=1, tiled=True)  30 us
    pallas_call x1, Pallas kernels, run_forward(): pl.pallas_call(attention_forward, out_shape=(jax.ShapeDtypeStruct((pairs,...  28.3 us
  transfers between devices with their start and end apart: 14, of which 7 were waited for; matrix products, arithmetic and copies ran while one was open for 4% of the time, Pallas kernels for 32%

profile of v2, /device:TPU:0, one launch (start us, length us, event | category | flops | bytes accessed | tf_op | source)
XLA Modules:
  0.0 544.0 jit_solution(3893723546583016735)
XLA Ops:
  8.0 4.1 collective-permute-start
  12.1 23.4 %collective-permute-done = bf16[1,512,512]{2,1,0:T(8,128)(2,1)S(1)} collective-permute-done((bf16[1,512,512]{2,1,0:T(8,128)(2,1)}, bf16[1,512,512]{2,1,0:T(8,128)(2,1)S(1)}, u32[]{:S(2)}, u32[]{:S(2)}) %collective-permute-start) | collective-permute-done | bytes 524320 | tf_op jit(solution)/shard_map/ppermute | solution.py:1025
  37.2 25.4 %collective-permute-done.1 = bf16[1,512,512]{2,1,0:T(8,128)(2,1)S(1)} collective-permute-done((bf16[1,512,512]{2,1,0:T(8,128)(2,1)}, bf16[1,512,512]{2,1,0:T(8,128)(2,1)S(1)}, u32[]{:S(2)}, u32[]{:S(2)}) %collective-permute-start.1) | collective-permute-done | bytes 524320 | tf_op jit(solution)/shard_map/ppermute | solution.py:1025
  64.4 39.5 %gather_weights.1 = (bf16[4,512,512]{2,1,0:T(8,128)(2,1)S(1)}, bf16[1280,512]{1,0:T(8,128)(2,1)S(1)}) custom-call(bf16[64,512]{1,0:T(8,128)(2,1)S(1)} %pad_maximum_fusion.3.wp_ref, bf16[768,512]{1,0:T(8,128)(2,1)S(1)} %copy-done.9), custom_call_target="tpu_custom_call" | custom-call | tf_op jit(solution)/shard_map/gather_weights/pallas_call | solution.py:562
  103.9 1.3 copy-done.3
  105.8 28.3 %attention_forward.1 = (bf16[4,1280,384]{2,1,0:T(8,128)(2,1)}, bf16[768,512]{1,0:T(8,128)(2,1)S(1)}, f32[768,512]{1,0:T(8,128)}, bf16[768,512]{1,0:T(8,128)(2,1)...) custom-call(bf16[1280,512]{1,0:T(8,128)(2,1)S(1)} %get-tuple-element.35.x_ref, ...), custom_call_target="tpu_custom_call" | custom-call | tf_op jit(solution)/shard_map/attention_forward/pallas_call | solution.py:683
  134.1 0.9 copy-done.5
  135.0 0.9 copy-done.8
  138.0 4.6 pad_maximum_fusion.w1_ref
  142.6 30.0 %all-gather.11.cloned.1.call-done = bf16[1,2048,512]{2,1,0:T(8,128)(2,1)} async-done(((bf16[1,512,512]{2,1,0:T(8,128)(2,1)}), bf16[1,2048,512]{2,1,0:T(8,128)(2,1)}) %all-gather.11.cloned.1.call-update) | async-done | bytes 2097168 | tf_op jit(solution)/shard_map/all_gather | solution.py:1027
  172.7 4.6 pad_maximum_fusion.1.w2_ref
  177.3 164.9 %experts.1 = (bf16[2,2048,512]{2,1,0:T(8,128)(2,1)}, bf16[2,2048,512]{2,1,0:T(8,128)(2,1)}, bf16[4,2,512,384]{3,2,1,0:T(8,128)(2,1)}, bf16[4,2,512,384]{3,2,1,0:T(8,128)(2,1)}, f32[4,8,384]{2,1,0:T(8,128)}) custom-call(bf16[768,512]{1,0:T(8,128)(2,1)} %copy-done.5, bf16[768,512]{1,0:T(8,128)(2,1)} %g_ref.3, f32[16,768]{1,0:T(8,128)} %copy-done.14, ...), custom_call_target="tpu_custom_call" | custom-call | tf_op jit(solution)/shard_map/experts/pallas_call | solution.py:898
  342.2 4.5 slice_bitcast_fusion.1
  346.8 4.5 slice_bitcast_fusion.3
  352.8 14.0 %combine.1 = (bf16[768,512]{1,0:T(8,128)(2,1)}, f32[768,512]{1,0:T(8,128)}, bf16[768,512]{1,0:T(8,128)(2,1)}, f32[8,512]{1,0:T(8,128)}, f32[128,512]{1,0:T(8,128)}, /*index=5*/f32[30,128]{1,0:T(8,128)}) custom-call(bf16[4,2,512,384]{3,2,1,0:T(8,128)(2,1)} %get-tuple-element.39.ret_g, bf16[4,2,512,384]{3,2,1,0:T(8,128)(2,1)} %get-tuple-element.40.ret_p, ...), custom_call_target="tpu_custom_call" | custom-call | tf_op jit(solution)/shard_map/combine/pallas_call | solution.py:1003
  366.8 1.1 fusion
  367.9 1.5 collective-permute-start.2
  369.4 1.5 collective-permute-start.3
  370.8 0.8 copy.50
  372.4 0.8 fusion.2
  373.2 7.4 %collective-permute-done.2 = bf16[256,512]{1,0:T(8,128)(2,1)S(1)} collective-permute-done((bf16[256,512]{1,0:T(8,128)(2,1)S(1)}, bf16[256,512]{1,0:T(8,128)(2,1)S(1)}, u32[]{:S(2)}, u32[]{:S(2)}) %collective-permute-start.2) | collective-permute-done | bytes 262176 | tf_op jit(solution)/shard_map/ppermute | solution.py:1077
  380.6 7.8 %collective-permute-done.3 = bf16[256,512]{1,0:T(8,128)(2,1)S(1)} collective-permute-done((bf16[256,512]{1,0:T(8,128)(2,1)S(1)}, bf16[256,512]{1,0:T(8,128)(2,1)S(1)}, u32[]{:S(2)}, u32[]{:S(2)}) %collective-permute-start.3) | collective-permute-done | bytes 262176 | tf_op jit(solution)/shard_map/ppermute | solution.py:1078
  388.4 2.3 pad_maximum_fusion.2.gatt_ref
  390.7 58.2 %attention_backward.1 = (bf16[4,512,512]{2,1,0:T(8,128)(2,1)}, bf16[768,512]{1,0:T(8,128)(2,1)}, f32[8,512]{1,0:T(8,128)}) custom-call(bf16[1280,512]{1,0:T(8,128)(2,1)} %copy-done.4, bf16[4,512,512]{2,1,0:T(8,128)(2,1)} %copy-done.3, s32[1,1280]{1,0:T(1,128)} %copy-done.15, s32[1280,1]{1,0:T(8,128)} %copy-done.2, f32[2,512]{1,0:T(2,128)} %gain_ref.5, ...), custom_call_target="tpu_custom_call" | custom-call | tf_op jit(solution)/shard_map/attention_backward/pallas_call | solution.py:706
  449.8 1.6 copy-done.6
  451.4 33.2 %reduce_all.1 = (f32[64,512]{1,0:T(8,128)S(1)}, f32[24,512]{1,0:T(8,128)S(1)}) custom-call(bf16[4,4,2,64,512]{4,3,2,1,0:T(8,128)(2,1)S(1)} %bitcast.29, f32[24,512]{1,0:T(8,128)S(1)} %concatenate.19.small_ref), custom_call_target="tpu_custom_call" | custom-call | tf_op jit(solution)/shard_map/reduce_all/pallas_call | solution.py:645
  485.1 1.9 collective-permute-start.5
  487.7 1.0 collective-permute-start.4
  490.5 32.8 %collective-permute-done.5 = bf16[512,512]{1,0:T(8,128)(2,1)S(1)} collective-permute-done((bf16[512,512]{1,0:T(8,128)(2,1)}, bf16[512,512]{1,0:T(8,128)(2,1)S(1)}, u32[]{:S(2)}, u32[]{:S(2)}) %collective-permute-start.5) | collective-permute-done | bytes 524320 | tf_op jit(solution)/shard_map/ppermute | solution.py:1036
  523.3 2.2 add_bitcast_fusion
  525.5 9.1 %collective-permute-done.4 = bf16[512,512]{1,0:T(8,128)(2,1)S(1)} collective-permute-done((bf16[512,512]{1,0:T(8,128)(2,1)}, bf16[512,512]{1,0:T(8,128)(2,1)S(1)}, u32[]{:S(2)}, u32[]{:S(2)}) %collective-permute-start.4) | collective-permute-done | bytes 524320 | tf_op jit(solution)/shard_map/ppermute | solution.py:1036
  534.6 2.2 add_bitcast_fusion.1
  (98 shorter events, 12.8 us)
Async XLA Ops:
  7.2 57.2 %copy-start = (bf16[64,3,128]{2,0,1:T(8,128)(2,1)S(1)}, bf16[64,3,128]{2,0,1:T(8,128)(2,1)}, u32[]{:S(2)}) copy-start(bf16[64,3,128]{2,0,1:T(8,128)(2,1)} %param.19) | copy-start | bytes 147460
  7.2 56.3 %copy-start.24 = (s32[3,16]{1,0:T(4,128)S(1)}, s32[3,16]{1,0:T(4,128)}, u32[]{:S(2)}) copy-start(s32[3,16]{1,0:T(4,128)} %param.14) | copy-start | bytes 580
  7.2 56.6 %copy-start.21 = (bf16[512,8]{0,1:T(8,128)(2,1)S(1)}, bf16[512,8]{0,1:T(8,128)(2,1)}, u32[]{:S(2)}) copy-start(bf16[512,8]{0,1:T(8,128)(2,1)} %param.21) | copy-start | bytes 24580
  7.2 56.8 %copy-start.23 = (f32[30,8]{0,1:T(8,128)S(1)}, f32[30,8]{0,1:T(8,128)}, u32[]{:S(2)}) copy-start(f32[30,8]{0,1:T(8,128)} %param.22) | copy-start | bytes 2884
  7.2 56.8 %copy-start.25 = (s32[3,16]{1,0:T(4,128)S(1)}, s32[3,16]{1,0:T(4,128)}, u32[]{:S(2)}) copy-start(s32[3,16]{1,0:T(4,128)} %param.15) | copy-start | bytes 580
  7.2 56.9 %copy-start.22 = (s32[768,2]{0,1:T(2,128)S(1)}, s32[768,2]{0,1:T(2,128)}, u32[]{:S(2)}) copy-start(s32[768,2]{0,1:T(2,128)} %param.16) | copy-start | bytes 18436
  7.2 57.2 %copy-start.20 = (bf16[64,128]{1,0:T(8,128)(2,1)S(1)}, bf16[64,128]{1,0:T(8,128)(2,1)}, u32[]{:S(2)}) copy-start(bf16[64,128]{1,0:T(8,128)(2,1)} %param.20) | copy-start | bytes 49156
  7.3 57.2 %copy-start.9 = (bf16[768,512]{1,0:T(8,128)(2,1)S(1)}, bf16[768,512]{1,0:T(8,128)(2,1)}, u32[]{:S(2)}) copy-start(bf16[768,512]{1,0:T(8,128)(2,1)} %x_ref.1) | copy-start | bytes 2359300
  7.3 130.7 %all-gather.5.cloned.1.call-start = ((), (), s32[]{:S(2)}) async-start(), calls=%async_computation.4 | async-start | bytes 2621440 | tf_op jit(solution)/shard_map/all_gather | solution.py:1026
  8.0 130.0 %all-gather.7.cloned.1.call-start = ((), (), s32[]{:S(2)}) async-start(), calls=%async_computation.5 | async-start | bytes 2621440 | tf_op jit(solution)/shard_map/all_gather | solution.py:1027
  8.0 27.5 %collective-permute-start = (bf16[1,512,512]{2,1,0:T(8,128)(2,1)}, bf16[1,512,512]{2,1,0:T(8,128)(2,1)S(1)}, u32[]{:S(2)}, u32[]{:S(2)}) collective-permute-start(bf16[1,512,512]{2,1,0:T(8,128)(2,1)} %param.23), channel_id=1, source_target_pairs={{0,4},{1,5},{2,6},{3,7},{4,0},{5,1},{6,2},{7,3},{8,12},{9,13},{10,... | collective-permute-start | bytes 1572872 | tf_op jit(solution)/shard_map/ppermute | solution.py:1025
  35.5 70.2 %copy-start.16 = (f32[2,512]{1,0:T(2,128)S(1)}, f32[2,512]{1,0:T(2,128)}, u32[]{:S(2)}) copy-start(f32[2,512]{1,0:T(2,128)} %gain_ref.5) | copy-start | bytes 12292
  35.5 70.3 %copy-start.17 = (f32[2,512]{1,0:T(2,128)S(1)}, f32[2,512]{1,0:T(2,128)}, u32[]{:S(2)}) copy-start(f32[2,512]{1,0:T(2,128)} %bias_ref.3) | copy-start | bytes 12292
  36.3 106.3 %all-gather.9.cloned.1.call-start = ((), (), s32[]{:S(2)}) async-start(), calls=%async_computation.6 | async-start | bytes 2621440 | tf_op jit(solution)/shard_map/all_gather | solution.py:1026
  37.1 135.6 %all-gather.11.cloned.1.call-start = ((), (), s32[]{:S(2)}) async-start(), calls=%async_computation.7 | async-start | bytes 2621440 | tf_op jit(solution)/shard_map/all_gather | solution.py:1027
  37.1 25.5 %collective-permute-start.1 = (bf16[1,512,512]{2,1,0:T(8,128)(2,1)}, bf16[1,512,512]{2,1,0:T(8,128)(2,1)S(1)}, u32[]{:S(2)}, u32[]{:S(2)}) collective-permute-start(bf16[1,512,512]{2,1,0:T(8,128)(2,1)} %param.24), channel_id=1, source_target_pairs={{0,4},{1,5},{2,6},{3,7},{4,0},{5,1},{6,2},{7,3},{8,12},{9,13},{10,... | collective-permute-start | bytes 1572872 | tf_op jit(solution)/shard_map/ppermute | solution.py:1025
  63.5 421.7 %reduce-scatter.11.cloned.1.call-start = ((), (), s32[]{:S(2)}) async-start(), calls=%async_computation.11 | async-start | bytes 2621440 | tf_op jit(solution)/shard_map/reduce_scatter | solution.py:1036
  64.2 69.9 %copy-start.12 = (s32[48,1]{1,0:T(8,128)}, s32[48,1]{1,0:T(8,128)S(1)}, u32[]{:S(2)}) copy-start(s32[48,1]{1,0:T(8,128)S(1)} %reshape.101.task_col) | copy-start | bytes 580
  105.3 28.8 %copy-start.4 = (bf16[1280,512]{1,0:T(8,128)(2,1)}, bf16[1280,512]{1,0:T(8,128)(2,1)S(1)}, u32[]{:S(2)}) copy-start(bf16[1280,512]{1,0:T(8,128)(2,1)S(1)} %get-tuple-element.35.x_ref) | copy-start | bytes 3932164
  105.3 28.8 %copy-start.7 = (bf16[512,128]{1,0:T(8,128)(2,1)}, bf16[512,128]{1,0:T(8,128)(2,1)S(1)}, u32[]{:S(2)}) copy-start(bf16[512,128]{1,0:T(8,128)(2,1)S(1)} %pad.12.router_ref) | copy-start | bytes 393220
  105.3 28.7 %copy-start.13 = (f32[30,128]{1,0:T(8,128)}, f32[30,128]{1,0:T(8,128)S(1)}, u32[]{:S(2)}) copy-start(f32[30,128]{1,0:T(8,128)S(1)} %pad.13.table_ref) | copy-start | bytes 46084
  105.5 28.6 %copy-start.15 = (s32[1,1280]{1,0:T(1,128)}, s32[1,1280]{1,0:T(1,128)S(1)}, u32[]{:S(2)}) copy-start(s32[1,1280]{1,0:T(1,128)S(1)} %compare_select_fusion.seg_row) | copy-start | bytes 15364
  105.8 28.4 %copy-start.2 = (s32[1280,1]{1,0:T(8,128)}, s32[1280,1]{1,0:T(8,128)S(1)}, u32[]{:S(2)}) copy-start(s32[1280,1]{1,0:T(8,128)S(1)} %reshape_select_fusion.seg_col) | copy-start | bytes 15364
  346.7 141.0 %reduce-scatter.7.cloned.1.call-start = ((), (), s32[]{:S(2)}) async-start(), calls=%async_computation.9 | async-start | bytes 2621440 | tf_op jit(solution)/shard_map/reduce_scatter | solution.py:1036
  351.3 139.2 %reduce-scatter.9.cloned.1.call-start = ((), (), s32[]{:S(2)}) async-start(), calls=%async_computation.10 | async-start | bytes 2621440 | tf_op jit(solution)/shard_map/reduce_scatter | solution.py:1035
  352.1 173.4 %reduce-scatter.5.cloned.1.call-start = ((), (), s32[]{:S(2)}) async-start(), calls=%async_computation.8 | async-start | bytes 2621440 | tf_op jit(solution)/shard_map/reduce_scatter | solution.py:1035
  367.9 12.7 %collective-permute-start.2 = (bf16[256,512]{1,0:T(8,128)(2,1)S(1)}, bf16[256,512]{1,0:T(8,128)(2,1)S(1)}, u32[]{:S(2)}, u32[]{:S(2)}) collective-permute-start(bf16[256,512]{1,0:T(8,128)(2,1)S(1)} %get-tuple-element.94), channel_id=1, source_target_pairs={{0,8},{8,16},{16,24},{24,0},{1,9},{9,17},{17,25},{25,1},{2,10},{10... | collective-permute-start | bytes 786440 | tf_op jit(solution)/shard_map/ppermute | solution.py:1077
  369.4 19.0 %collective-permute-start.3 = (bf16[256,512]{1,0:T(8,128)(2,1)S(1)}, bf16[256,512]{1,0:T(8,128)(2,1)S(1)}, u32[]{:S(2)}, u32[]{:S(2)}) collective-permute-start(bf16[256,512]{1,0:T(8,128)(2,1)S(1)} %get-tuple-element.95), channel_id=1, source_target_pairs={{0,24},{8,0},{16,8},{24,16},{1,25},{9,1},{17,9},{25,17},{2,26},{10... | collective-permute-start | bytes 786440 | tf_op jit(solution)/shard_map/ppermute | solution.py:1078
  449.8 1.6 copy-start.6
  485.1 38.2 %collective-permute-start.5 = (bf16[512,512]{1,0:T(8,128)(2,1)}, bf16[512,512]{1,0:T(8,128)(2,1)S(1)}, u32[]{:S(2)}, u32[]{:S(2)}) collective-permute-start(bf16[512,512]{1,0:T(8,128)(2,1)} %reduce-scatter.11.cloned.1.call-done), channel_id=1, source_target_pairs={{0,4},{1,5},{2,6},{3,7},{4,0},{5,1},{6,2},{7,3},{8,12},{9,13},{10,... | collective-permute-start | bytes 1572872 | tf_op jit(solution)/shard_map/ppermute | solution.py:1036
  487.7 46.9 %collective-permute-start.4 = (bf16[512,512]{1,0:T(8,128)(2,1)}, bf16[512,512]{1,0:T(8,128)(2,1)S(1)}, u32[]{:S(2)}, u32[]{:S(2)}) collective-permute-start(bf16[512,512]{1,0:T(8,128)(2,1)} %reduce-scatter.7.cloned.1.call-done), channel_id=1, source_target_pairs={{0,4},{1,5},{2,6},{3,7},{4,0},{5,1},{6,2},{7,3},{8,12},{9,13},{10,... | collective-permute-start | bytes 1572872 | tf_op jit(solution)/shard_map/ppermute | solution.py:1036
  489.9 46.8 %copy-start.1 = (bf16[64,3,128]{2,0,1:T(8,128)(2,1)S(1)}, bf16[64,3,128]{2,0,1:T(8,128)(2,1)}, u32[]{:S(2)}) copy-start(bf16[64,3,128]{2,0,1:T(8,128)(2,1)} %param.19) | copy-start | bytes 147460
  (8 other events, 6.8 us)
Sparse Core Ops, SparseCore 0:
  9.9 38.0 all-gather.4
  50.4 47.3 all-gather.6
  99.6 35.4 all-gather.8
  137.4 35.2 all-gather.10
  346.8 39.9 reduce-scatter.10
  389.9 35.2 reduce-scatter.6
  428.1 40.7 reduce-scatter.8
  472.2 41.1 reduce-scatter.4
